TPU v7x, 256 devices: a whole 4x4x8 slice. The times are simulated.
256 devices in a mesh: tm: 128 (over x, z, y_hi, core), net: 2 (over y_lo).
Axes of the slice: x: 4, y: 4 (y_hi: 2, y_lo: 2; y = y_hi * 2 + y_lo), z: 8, core: 2. Of those that a mesh axis runs over, the one named last changes fastest.
Arguments:
- jacobian: bfloat16 [524288, 1024], P(('net', 'tm')), parts along dimension 0, may hold values from -24 to 24
- misfit: bfloat16 [524288], P(('net', 'tm')), parts along dimension 0, may hold values from -6 to 6
- taps: float32 [128], P('net'), parts along dimension 0, may hold values from -0.4 to 0.4
Outputs:
- fisher: float32 [2048, 1024], P(('net', 'tm')), parts along dimension 0
- newton: float32 [2048], P(('net', 'tm')), parts along dimension 0
There are 2 independent parts, one for each index of `net`. A program takes and returns all parts, laid end to end along the dimension named above; each array names one. Nothing has to cross between parts.
All inputs are finite; a program needn't handle non-finite values.
Results may differ from a plain program's by a relative error of at most 0.0039.
Values may be sent and summed in bfloat16 or wider, within the bound.
A program may use at most 64 MiB of HBM per device.

v0:
```python
import jax
import jax.numpy as jnp
from jax import lax
from jax.sharding import PartitionSpec as P


def passed_along(value, axis, steps):
    count = lax.axis_size(axis)
    initial, last = (max(0, -steps), min(count, count - steps))
    return lax.ppermute(value, axis, [(source, source + steps) for source in range(initial, last)])


def tap_matrix(coef, block, order):
    rows = jnp.arange(block, dtype=jnp.int32)[:, None]
    cols = jnp.arange(block + order, dtype=jnp.int32)[None, :]
    lag = rows + order - cols
    lags = jnp.arange(1, order + 1, dtype=jnp.int32)
    picked = jnp.sum(
        jnp.where(lag[:, :, None] == lags[None, None, :], coef[None, None, :], 0.0), axis=2
    )
    return jnp.where(lag == 0, 1.0, -picked)


def shards(jacobian, misfit, taps):
    rows_here, width = jacobian.shape
    order = taps.shape[0]
    block = min(128, rows_here)
    count = rows_here // block
    coef = taps.astype(jnp.bfloat16).astype(jnp.float32)
    matrix = tap_matrix(coef, block, order).astype(jnp.bfloat16)
    jac_tail, mis_tail = passed_along(
        (jacobian[rows_here - order :], misfit[rows_here - order :]), "tm", 1
    )
    jac_blocks = jacobian.reshape(count, block, width)
    prev = jnp.concatenate([jac_tail[None], jac_blocks[:-1, block - order :]], axis=0)
    whitened = jnp.einsum(
        "ij,bjp->bip", matrix[:, :order], prev, preferred_element_type=jnp.float32
    )
    whitened = whitened + jnp.einsum(
        "ij,bjp->bip", matrix[:, order:], jac_blocks, preferred_element_type=jnp.float32
    )
    whitened = whitened.astype(jnp.bfloat16).reshape(rows_here, width)
    mis_blocks = misfit.reshape(count, block)
    mis_prev = jnp.concatenate([mis_tail[None], mis_blocks[:-1, block - order :]], axis=0)
    white_misfit = jnp.einsum(
        "ij,bj->bi", matrix[:, :order], mis_prev, preferred_element_type=jnp.float32
    )
    white_misfit = white_misfit + jnp.einsum(
        "ij,bj->bi", matrix[:, order:], mis_blocks, preferred_element_type=jnp.float32
    )
    white_misfit = white_misfit.astype(jnp.bfloat16).reshape(rows_here)
    total = rows_here * lax.axis_size("tm")
    owned = width // lax.axis_size("tm")
    grad_term = jnp.dot(white_misfit, whitened, preferred_element_type=jnp.float32)
    gram = lax.dot_general(
        whitened, whitened, (((0,), (0,)), ((), ())), preferred_element_type=jnp.float32
    )
    fisher_rows, grad_rows = (
        lax.psum_scatter(gram, "tm", scatter_dimension=0, tiled=True),
        lax.psum_scatter(grad_term, "tm", scatter_dimension=0, tiled=True),
    )
    fisher_rows = fisher_rows / total
    grad_rows = grad_rows / total
    first = lax.axis_index("tm") * owned
    wanted = first + jnp.arange(owned, dtype=jnp.int32)
    select = jnp.arange(width, dtype=jnp.int32)[None, :] == wanted[:, None]
    diagonal = jnp.sum(jnp.where(select, fisher_rows, 0.0), axis=1)
    return (fisher_rows, grad_rows / diagonal)


def solution(mesh):
    in_specs = (P(("net", "tm"), None), P(("net", "tm")), P("net"))
    out_specs = (P(("net", "tm"), None), P(("net", "tm")))
    return jax.shard_map(shards, mesh=mesh, in_specs=in_specs, out_specs=out_specs, check_vma=False)
```

profile of v0, /device:TPU:1, one launch (start us, length us, event | category | flops | bytes accessed | tf_op | source)
XLA Modules:
  0.0 699.8 jit_solution(10020736618271755107)
XLA Ops:
  7.2 0.0 reduce-scatter.2.cloned.1.call-start
  7.2 0.9 slice.20
  8.1 6.2 collective-permute-start
  14.4 0.7 convert_convert_fusion
  15.0 1.5 select_reduce_fusion
  16.6 4.0 fusion.6
  20.5 1.7 slice.26
  22.2 0.0 collective-permute-done
  22.3 1.4 fusion
  23.6 0.0 copy-start
  23.6 2.0 copy-done
  25.6 6.1 convolution_bitcast_fusion
  31.7 0.0 copy-start.1
  31.7 0.0 copy-start.2
  31.7 0.0 reduce-scatter.2.cloned.1.call-update
  31.7 0.7 copy-done.1
  32.4 0.1 slice.24
  32.4 1.9 collective-permute-start.1
  34.4 0.1 slice.29
  34.5 0.0 copy-done.2
  34.5 0.6 dynamic-slice
  35.0 0.1 convolution_bitcast_fusion.1
  35.8 0.0 collective-permute-done.1
  35.8 0.1 fusion.5
  36.0 3.4 fusion.13
  39.3 326.7 %all-reduce = f32[1024]{0:T(1024)S(1)} all-reduce(f32[1024]{0:T(1024)S(1)} %bitcast.33), channel_id=3, replica_groups=mesh['tm'=128,'net'=2] {'tm'}, use_global_device_ids=true, to_apply=%region_2.3.clone | all-reduce | flops 1024 | bytes 8192
  366.0 324.9 %reduce-scatter.2.cloned.1.call-done = f32[8,1024]{1,0:T(8,128)} async-done(((f32[1024,1024]{1,0:T(8,128)}), f32[8,1024]{1,0:T(8,128)}) %reduce-scatter.2.cloned.1.call-update) | async-done | bytes 32784 | tf_op jit(solution)/shard_map/reduce_scatter | solution.py:59
  690.9 1.5 select_reduce_fusion.1
  692.4 0.6 fusion.18
  (5 shorter events, 0.0 us)
Async XLA Ops:
  7.2 683.7 %reduce-scatter.2.cloned.1.call-start = ((), (), s32[]{:S(2)}) async-start(), calls=%async_computation.1 | async-start | bytes 4227072 | tf_op jit(solution)/shard_map/reduce_scatter | solution.py:59
  8.1 14.1 %collective-permute-start = (bf16[64,1024]{1,0:T(8,128)(2,1)S(1)}, bf16[64,1024]{1,0:T(8,128)(2,1)S(1)}, u32[]{:S(2)}, u32[]{:S(2)}) collective-permute-start(bf16[64,1024]{1,0:T(8,128)(2,1)S(1)} %slice.20), channel_id=1, source_target_pairs={{0,2},{2,4},{4,6},{6,8},{8,10},{10,12},{12,14},{14,16},{16,18},{18... | collective-permute-start | bytes 393224 | tf_op jit(solution)/shard_map/ppermute | solution.py:10
  23.6 2.0 copy-start
  31.7 0.7 copy-start.1
  31.7 2.8 copy-start.2
  32.4 3.4 collective-permute-start.1
Sparse Core Ops, SparseCore 0:
  31.8 658.9 reduce-scatter.1
where the time goes:
time: 706 us; the launch traced here: 700 us
  blocking collectives  327 us (46%)
  waiting for transfers between devices  325 us (46%)
  matrix products  15 us (2%)
  between operations  14.8 us (2%)
  starting transfers between devices  8.16 us (1%)
    unnamed x1, blocking collectives  327 us
    reduce_scatter x1, waiting for transfers between devices, shards(): lax.psum_scatter(gram, 'tm', scatter_dimension=0, tiled=True)  325 us
  transfers between devices with their start and end apart: 3, of which 1 were waited for; matrix products, arithmetic and copies ran while one was open for 2% of the time, Pallas kernels for 0%

commit v1 on v0

v1 whole, which is shorter than its diff:
```python
import jax
import jax.numpy as jnp
from jax import lax
from jax.experimental import pallas as pl
from jax.experimental.pallas import tpu as pltpu
from jax.sharding import PartitionSpec as P

NX, NZ, NY, NC = 4, 8, 2, 2
NU = NX * NY
OWNERS = NX * NZ * NY * NC
MESH = pl.DeviceIdType.MESH
BF16, F32 = jnp.bfloat16, jnp.float32

ROWS, WIDTH, ORDER = 2048, 1024, 64
BLOCK = 192
CHUNKS = 4
ACOLS = 256
BCOLS = WIDTH - ACOLS
AHALF, BHALF = ACOLS // 2, BCOLS // 2
TOTAL = ROWS * OWNERS
XY_STEPS = [(2, 0), (2, 1), (1, 0), (3, 0), (1, 1), (3, 1), (0, 1)]
Z_STEPS = [4, 3, 5, 2, 6, 1, 7]


def position(x, z, y, c):
    return ((lax.rem(x, NX) * NZ + lax.rem(z, NZ)) * NY + lax.rem(y, NY)) * NC + lax.rem(c, NC)


def folded(rows):
    half = rows.shape[1] // 2
    return jnp.concatenate([rows[:, :half], rows[:, half:]], axis=0)


def unfolded(piece):
    return jnp.concatenate([piece[:8], piece[8:]], axis=1)


def kernel(
    jac, mis, taps, fisher, newton,
    xbuf, white, white_t, wm_rows, mis_tail,
    keep_a, keep_b, core_sa, core_sb, core_ra, core_rb,
    s1a, s1b, r1a, r1b, a2, b2, s2a, s2b, r2a, r2b,
    load_sem, halo_ss, halo_rs, core_ss, core_rs,
    s1a_ss, s1a_rs, s1b_ss, s1b_rs, s2a_ss, s2a_rs, s2b_ss, s2b_rs,
):
    me = lax.axis_index("tm")
    x, z, y, c = me // (NZ * NY * NC), (me // (NY * NC)) % NZ, (me // NC) % NY, me % NC
    sibling = position(x, z, y, c + 1)
    after, before = lax.rem(me + 1, OWNERS), lax.rem(me + OWNERS - 1, OWNERS)
    xy_dev = [position(x + dx, z, y + dy, c) for dx, dy in XY_STEPS]
    xy_own = [lax.rem(x + dx, NX) * NY + lax.rem(y + dy, NY) for dx, dy in XY_STEPS]
    z_dev = [position(x, z + dz, y, c) for dz in Z_STEPS]
    z_own = [lax.rem(z + dz, NZ) for dz in Z_STEPS]
    u = x * NY + y

    step_rows = ROWS // CHUNKS
    loads = []
    for i in reversed(range(CHUNKS)):
        load = pltpu.make_async_copy(
            jac.at[pl.ds(i * step_rows, step_rows)],
            xbuf.at[pl.ds(ORDER + i * step_rows, step_rows)],
            load_sem.at[i],
        )
        load.start()
        loads.append(load)
    loads = loads[::-1]

    barrier = pltpu.get_barrier_semaphore()
    partners = [sibling, after, before] + xy_dev + z_dev
    for device in partners:
        pl.semaphore_signal(barrier, inc=1, device_id={"tm": device}, device_id_type=MESH)

    coef = jnp.broadcast_to(taps[...].astype(BF16), (16, ORDER))
    lag_of = lax.broadcasted_iota(jnp.int32, (ORDER, 256), 0)
    lane_of = lax.broadcasted_iota(jnp.int32, (ORDER, 256), 1)
    flip = (lag_of + lane_of == ORDER - 1).astype(F32).astype(BF16)
    first = jnp.dot(coef, flip, preferred_element_type=F32)[:1]
    lane = lax.broadcasted_iota(jnp.int32, (1, 256), 1)
    first = jnp.where(lane == ORDER, 1.0, -first)
    matrix = pltpu.roll(jnp.broadcast_to(first, (BLOCK, 256)), 0, 1, stride=1, stride_axis=0).astype(BF16)
    mis_matrix = pltpu.roll(jnp.broadcast_to(first, (128, 256)), ORDER, 1, stride=1, stride_axis=0).astype(BF16)

    pl.semaphore_wait(barrier, len(partners))

    halo = pltpu.make_async_remote_copy(
        src_ref=jac.at[pl.ds(ROWS - ORDER, ORDER)], dst_ref=xbuf.at[pl.ds(0, ORDER)],
        send_sem=halo_ss.at[0], recv_sem=halo_rs.at[0], device_id={"tm": after}, device_id_type=MESH,
    )
    mis_halo = pltpu.make_async_remote_copy(
        src_ref=mis, dst_ref=mis_tail,
        send_sem=halo_ss.at[1], recv_sem=halo_rs.at[1], device_id={"tm": after}, device_id_type=MESH,
    )

    @pl.when(me < OWNERS - 1)
    def _():
        halo.start()
        mis_halo.start()

    def whiten(start, rows):
        out = jnp.dot(
            matrix[:rows, : rows + ORDER], xbuf[start : start + rows + ORDER], preferred_element_type=F32
        )
        white[start : start + rows] = out.astype(BF16)

    starts = list(range(0, ROWS, BLOCK))
    ready = CHUNKS
    for start in starts[::-1]:
        rows = min(BLOCK, ROWS - start)
        lowest = max(0, start - ORDER)
        while ready * step_rows > lowest:
            ready -= 1
            loads[ready].wait()
        if start == 0:

            @pl.when(me > 0)
            def _():
                halo.wait_recv()
                mis_halo.wait_recv()

            @pl.when(me == 0)
            def _():
                xbuf[:ORDER] = jnp.zeros((ORDER, WIDTH), BF16)
                mis_tail[...] = jnp.zeros_like(mis_tail)

        whiten(start, rows)

    here = mis[...].astype(F32)
    row_of = lax.broadcasted_iota(jnp.int32, (16, 128), 0)
    previous = jnp.where(
        row_of == 0, pltpu.roll(mis_tail[...].astype(F32), 1, 0), pltpu.roll(here, 1, 0)
    )
    both = jnp.concatenate([previous, here], axis=1).astype(BF16)
    white_mis = lax.dot_general(both, mis_matrix, (((1,), (1,)), ((), ())), preferred_element_type=F32)
    for i in range(16):
        wm_rows[:, i * 128 : (i + 1) * 128] = jnp.broadcast_to(white_mis[i : i + 1], (16, 128)).astype(BF16)

    for i in range(ROWS // 256):
        white_t[:, i * 256 : (i + 1) * 256] = white[i * 256 : (i + 1) * 256].T

    mine_first = c == 0

    def split(rows, grad, owner, offset, keep, send, index):
        pair = []
        for side in range(NC):
            part = rows[side * 8 : side * 8 + 8]
            r = lax.broadcasted_iota(jnp.int32, part.shape, 0)
            col = lax.broadcasted_iota(jnp.int32, part.shape, 1)
            beside = col == (owner + side) * 8 - offset + lax.rem(r + 1, 8)
            pair.append(folded(jnp.where(beside, jnp.broadcast_to(grad, part.shape), part)))
        keep[index] = jnp.where(mine_first, pair[0], pair[1])
        send[index] = jnp.where(mine_first, pair[1], pair[0]).astype(BF16)

    def to_sibling(src, dst, k):
        return pltpu.make_async_remote_copy(
            src_ref=src, dst_ref=dst, send_sem=core_ss.at[k], recv_sem=core_rs.at[k],
            device_id={"tm": sibling}, device_id_type=MESH,
        )

    copies = []
    for xo in range(NX):
        lhs = white_t[xo * 256 : (xo + 1) * 256]
        if xo == 0:
            lhs = jnp.concatenate([lhs, wm_rows[...]], axis=0)
        out = jnp.dot(lhs, white[:, :ACOLS], preferred_element_type=F32)
        if xo == 0:
            grad = out[256:257]
        for zo in range(NZ):
            for yo in range(NY):
                row = (zo * NY + yo) * NC * 8
                split(
                    out[row : row + 16], grad, xo * 32 + (zo * NY + yo) * NC, 0,
                    keep_a, core_sa, zo * NU + xo * NY + yo,
                )
    core_a = to_sibling(core_sa, core_ra, 0)
    core_a.start()
    copies.append(core_a)

    stage1a, stage1b, core_b = [], [], []

    def send_a():
        core_a.wait_recv()
        s1a[...] = (keep_a[...] + core_ra[...].astype(F32)).astype(BF16)
        for k, (device, own) in enumerate(zip(z_dev, z_own)):
            copy = pltpu.make_async_remote_copy(
                src_ref=s1a.at[pl.ds(own * NU, NU)], dst_ref=r1a.at[k],
                send_sem=s1a_ss.at[k], recv_sem=s1a_rs.at[k], device_id={"tm": device}, device_id_type=MESH,
            )
            copy.start()
            stage1a.append(copy)

    def send_b(step):
        dx = X_ORDER[step]
        xo = lax.rem(x + dx, NX)
        core_b[step].wait_recv()
        span = pl.ds(xo * 16, 16)
        s1b[span] = (keep_b[span] + core_rb[span].astype(F32)).astype(BF16)
        for k, (device, own) in enumerate(zip(xy_dev, xy_own)):
            if XY_STEPS[k][0] == dx:
                copy = pltpu.make_async_remote_copy(
                    src_ref=s1b.at[pl.ds(own * NZ, NZ)], dst_ref=r1b.at[k],
                    send_sem=s1b_ss.at[k], recv_sem=s1b_rs.at[k], device_id={"tm": device}, device_id_type=MESH,
                )
                copy.start()
                stage1b.append((k, copy))

    X_ORDER = [2, 1, 3, 0]
    for step, dx in enumerate(X_ORDER):
        xo = lax.rem(x + dx, NX)
        lhs = jnp.concatenate([white_t[pl.ds(pl.multiple_of(xo * 256, 256), 256)], wm_rows[...]], axis=0)
        out = jnp.dot(lhs, white[:, ACOLS:], preferred_element_type=F32)
        grad = out[256:257]
        for zo in range(NZ):
            for yo in range(NY):
                row = (zo * NY + yo) * NC * 8
                split(
                    out[row : row + 16], grad, xo * 32 + (zo * NY + yo) * NC, ACOLS,
                    keep_b, core_sb, (xo * NY + yo) * NZ + zo,
                )
        span = pl.ds(xo * 16, 16)
        copy = to_sibling(core_sb.at[span], core_rb.at[span], 1 + step)
        copy.start()
        core_b.append(copy)
        if step == 0:
            send_a()
        else:
            send_b(step - 1)
    send_b(NX - 1)

    span = pl.ds(z * NU, NU)
    total = keep_a[span] + core_ra[span].astype(F32)
    for k, copy in enumerate(stage1a):
        copy.wait_recv()
        total = total + r1a[k].astype(F32)
    a2[...] = total
    s2a[...] = total.astype(BF16)
    stage2a = []
    for k, (device, own) in enumerate(zip(xy_dev, xy_own)):
        copy = pltpu.make_async_remote_copy(
            src_ref=s2a.at[own], dst_ref=r2a.at[k],
            send_sem=s2a_ss.at[k], recv_sem=s2a_rs.at[k], device_id={"tm": device}, device_id_type=MESH,
        )
        copy.start()
        stage2a.append(copy)

    span = pl.ds(u * NZ, NZ)
    b2[...] = keep_b[span] + core_rb[span].astype(F32)
    for k, copy in stage1b:
        copy.wait_recv()
        b2[...] += r1b[k].astype(F32)
    s2b[...] = b2[...].astype(BF16)
    stage2b = []
    for k, (device, own) in enumerate(zip(z_dev, z_own)):
        copy = pltpu.make_async_remote_copy(
            src_ref=s2b.at[own], dst_ref=r2b.at[k],
            send_sem=s2b_ss.at[k], recv_sem=s2b_rs.at[k], device_id={"tm": device}, device_id_type=MESH,
        )
        copy.start()
        stage2b.append(copy)

    last_a, last_b = a2[u], b2[z]
    for k, copy in enumerate(stage2a):
        copy.wait_recv()
        last_a = last_a + r2a[k].astype(F32)
    for k, copy in enumerate(stage2b):
        copy.wait_recv()
        last_b = last_b + r2b[k].astype(F32)
    rows = jnp.concatenate([unfolded(last_a), unfolded(last_b)], axis=1)

    r = lax.broadcasted_iota(jnp.int32, rows.shape, 0)
    col = lax.broadcasted_iota(jnp.int32, rows.shape, 1) - me * 8
    beside, on = col == lax.rem(r + 1, 8), col == r
    grad = pltpu.roll(jnp.sum(jnp.where(beside, rows, 0.0), axis=1, keepdims=True) + jnp.zeros((8, 128), F32), 1, 0)
    diagonal = jnp.sum(jnp.where(on, rows, 0.0), axis=1, keepdims=True)
    mirrored = jnp.sum(jnp.where(on, pltpu.roll(rows, 7, 0), 0.0), axis=1, keepdims=True)
    fisher[...] = jnp.where(beside, mirrored, rows) * (1.0 / TOTAL)
    ratio = grad / diagonal
    r8 = lax.broadcasted_iota(jnp.int32, (8, 128), 0)
    c8 = lax.broadcasted_iota(jnp.int32, (8, 128), 1)
    newton[...] = jnp.sum(jnp.where(r8 == c8, ratio, 0.0), axis=0, keepdims=True)[:, :8]

    @pl.when(me < OWNERS - 1)
    def _():
        halo.wait_send()
        mis_halo.wait_send()

    for copy in copies + core_b + stage1a + [copy for _, copy in stage1b] + stage2a + stage2b:
        copy.wait_send()


def shards(jacobian, misfit, taps):
    dma = pltpu.SemaphoreType.DMA
    vmem = pl.BlockSpec(memory_space=pltpu.VMEM)
    fisher, newton = pl.pallas_call(
        kernel,
        out_shape=(jax.ShapeDtypeStruct((8, WIDTH), F32), jax.ShapeDtypeStruct((1, 8), F32)),
        in_specs=[pl.BlockSpec(memory_space=pl.ANY), vmem, vmem],
        out_specs=(vmem, vmem),
        scratch_shapes=[
            pltpu.VMEM((ROWS + ORDER, WIDTH), BF16),
            pltpu.VMEM((ROWS, WIDTH), BF16),
            pltpu.VMEM((WIDTH, ROWS), BF16),
            pltpu.VMEM((16, ROWS), BF16),
            pltpu.VMEM((16, 128), BF16),
            pltpu.VMEM((64, 16, AHALF), F32),
            pltpu.VMEM((64, 16, BHALF), F32),
            pltpu.VMEM((64, 16, AHALF), BF16),
            pltpu.VMEM((64, 16, BHALF), BF16),
            pltpu.VMEM((64, 16, AHALF), BF16),
            pltpu.VMEM((64, 16, BHALF), BF16),
            pltpu.VMEM((64, 16, AHALF), BF16),
            pltpu.VMEM((64, 16, BHALF), BF16),
            pltpu.VMEM((7, 8, 16, AHALF), BF16),
            pltpu.VMEM((7, 8, 16, BHALF), BF16),
            pltpu.VMEM((8, 16, AHALF), F32),
            pltpu.VMEM((8, 16, BHALF), F32),
            pltpu.VMEM((8, 16, AHALF), BF16),
            pltpu.VMEM((8, 16, BHALF), BF16),
            pltpu.VMEM((7, 16, AHALF), BF16),
            pltpu.VMEM((7, 16, BHALF), BF16),
            dma((CHUNKS,)), dma((2,)), dma((2,)), dma((5,)), dma((5,)),
            dma((7,)), dma((7,)), dma((7,)), dma((7,)), dma((7,)), dma((7,)), dma((7,)), dma((7,)),
        ],
        compiler_params=pltpu.CompilerParams(
            collective_id=0, has_side_effects=True, vmem_limit_bytes=56 * 1024 * 1024
        ),
    )(jacobian, misfit.reshape(16, 128), taps.reshape(1, ORDER))
    return fisher, newton.reshape(8)


def solution(mesh):
    in_specs = (P(("net", "tm"), None), P(("net", "tm")), P("net"))
    out_specs = (P(("net", "tm"), None), P(("net", "tm")))
    return jax.shard_map(shards, mesh=mesh, in_specs=in_specs, out_specs=out_specs, check_vma=False)
```

time: 706 us -> 43.2 us (0.06)
  blocking collectives: 327 us -> 0 us
  waiting for transfers between devices: 325 us -> 0 us
  Pallas kernels: 0 us -> 39.8 us
  matrix products: 15 us -> 0 us
  between operations: 14.8 us -> 0.64 us
  starting transfers between devices: 8.16 us -> 0 us
    unnamed x1 -> x0, blocking collectives: 327 us -> none
    reduce_scatter x1 -> x0, waiting for transfers between devices: 325 us -> none  [shards(): lax.psum_scatter(gram, 'tm', scatter_dimension=0, tiled=True)]
    pallas_call x0 -> x1, Pallas kernels: none -> 39.8 us  [shards(): pl.pallas_call(kernel, out_shape=(jax.ShapeDtypeStruct((8, WIDTH), F32),...]
    dot_general x6 -> x0, matrix products: 15 us -> none  [the longest x1 6.08 us: shards(): lax.dot_general(whitened, whitened, (((0,), (0,)), ((), ())), preferred_e...]
    ppermute x2 -> x0, starting transfers between devices: 8.12 us -> none  [passed_along(): lax.ppermute(value, axis, [(source, source + steps) for source in range(i...]
  transfers between devices with their start and end apart: 3 -> 0, of which waited for: 1 -> 0; matrix products, arithmetic and copies ran while one was open for 2% -> 0% of each run, Pallas kernels for 0% -> 0%
where the time goes in v1:
time: 43.2 us; the launch traced here: 43 us
  Pallas kernels  39.8 us (92%)
  local copies, waits for them, and re-layouts  2.55 us (6%)
  between operations  0.64 us (1%)
    pallas_call x1, Pallas kernels, shards(): pl.pallas_call(kernel, out_shape=(jax.ShapeDtypeStruct((8, WIDTH), F32),...  39.8 us
    unnamed x2, local copies, waits for them, and re-layouts  2.55 us

profile of v1, /device:TPU:1, one launch (start us, length us, event | category | flops | bytes accessed | tf_op | source)
XLA Modules:
  0.0 43.0 jit_solution(4662012596862450501)
XLA Ops:
  0.6 39.8 %shard_map.50 = (f32[8,1024]{1,0:T(8,128)}, f32[1,8]{1,0:T(1,128)}) custom-call(bf16[2048,1024]{1,0:T(8,128)(2,1)} %jac.1, bf16[16,128]{1,0:T(8,128)(2,1)} %bitcast.3, f32[1,64]{1,0:T(1,128)} %bitcast.4), custom_call_target="tpu_custom_call" | custom-call | tf_op jit(solution)/shard_map/pallas_call | solution.py:293
  40.4 1.4 %copy.7 = f32[8,1024]{1,0:T(8,128)} copy(f32[8,1024]{1,0:T(8,128)} %get-tuple-element.8) | data formatting | bytes 65536
  41.8 1.2 %copy.8 = f32[8]{0:T(128)} copy(f32[8]{0:T(128)} %bitcast.5) | data formatting | bytes 64

commit v2 on v1

v2 whole, which is shorter than its diff:
```python
import jax
import jax.numpy as jnp
from jax import lax
from jax.experimental import pallas as pl
from jax.experimental.pallas import tpu as pltpu
from jax.sharding import PartitionSpec as P

NX, NZ, NY, NC = 4, 8, 2, 2
NU = NX * NY
OWNERS = NX * NZ * NY * NC
MESH = pl.DeviceIdType.MESH
BF16, F32 = jnp.bfloat16, jnp.float32

ROWS, WIDTH, ORDER = 2048, 1024, 64
BLOCK = 192
CHUNKS = 8
KROWS = 256
ACOLS = 256
BCOLS = WIDTH - ACOLS
AHALF, BHALF = ACOLS // 2, BCOLS // 2
TOTAL = ROWS * OWNERS
XY_STEPS = [(2, 0), (2, 1), (1, 0), (3, 0), (1, 1), (3, 1), (0, 1)]
Z_STEPS = [4, 3, 5, 2, 6, 1, 7]


def position(x, z, y, c):
    return ((lax.rem(x, NX) * NZ + lax.rem(z, NZ)) * NY + lax.rem(y, NY)) * NC + lax.rem(c, NC)


def folded(rows):
    half = rows.shape[1] // 2
    return jnp.concatenate([rows[:, :half], rows[:, half:]], axis=0)


def unfolded(piece):
    return jnp.concatenate([piece[:8], piece[8:]], axis=1)


def beside(base):
    r = lax.broadcasted_iota(jnp.int32, (8, 128), 0)
    lane = lax.broadcasted_iota(jnp.int32, (8, 128), 1) - base
    return lane == lax.rem(r + 1, 8), lane == lax.rem(r + 2, 8)


def two_terms(value):
    high = value.astype(BF16).astype(F32)
    return high, value - high


def place(tile, base, high, low):
    one, two = beside(base)
    return jnp.where(one, high, jnp.where(two, low, tile))


def split_again(tile, base):
    one, two = beside(base)
    high, low = two_terms(jnp.sum(jnp.where(one | two, tile, 0.0), axis=0, keepdims=True))
    return jnp.where(one, high, jnp.where(two, low, tile))


def kernel(
    jac, mis, taps, rows_out,
    xbuf, white, white_t, wm_rows, mis_tail, acc_a, acc_b,
    keep_a, keep_b, core_sa, core_sb, core_ra, core_rb,
    s1a, s1b, r1a, r1b, a2, b2, s2a, s2b, r2a, r2b,
    load_sem, halo_ss, halo_rs, core_ss, core_rs,
    s1a_ss, s1a_rs, s1b_ss, s1b_rs, s2a_ss, s2a_rs, s2b_ss, s2b_rs,
):
    me = lax.axis_index("tm")
    x, z, y, c = me // (NZ * NY * NC), (me // (NY * NC)) % NZ, (me // NC) % NY, me % NC
    sibling = position(x, z, y, c + 1)
    after, before = lax.rem(me + 1, OWNERS), lax.rem(me + OWNERS - 1, OWNERS)
    xy_dev = [position(x + dx, z, y + dy, c) for dx, dy in XY_STEPS]
    xy_own = [lax.rem(x + dx, NX) * NY + lax.rem(y + dy, NY) for dx, dy in XY_STEPS]
    z_dev = [position(x, z + dz, y, c) for dz in Z_STEPS]
    z_own = [lax.rem(z + dz, NZ) for dz in Z_STEPS]
    u = x * NY + y

    step_rows = ROWS // CHUNKS
    loads = []
    for i in reversed(range(CHUNKS)):
        load = pltpu.make_async_copy(
            jac.at[pl.ds(i * step_rows, step_rows)],
            xbuf.at[pl.ds(ORDER + i * step_rows, step_rows)],
            load_sem.at[i],
        )
        load.start()
        loads.append(load)
    loads = loads[::-1]

    barrier = pltpu.get_barrier_semaphore()
    partners = [sibling, after, before] + xy_dev + z_dev
    for device in partners:
        pl.semaphore_signal(barrier, inc=1, device_id={"tm": device}, device_id_type=MESH)

    coef = jnp.broadcast_to(taps[...].astype(BF16), (16, ORDER))
    lag_of = lax.broadcasted_iota(jnp.int32, (ORDER, 256), 0)
    lane_of = lax.broadcasted_iota(jnp.int32, (ORDER, 256), 1)
    flip = (lag_of + lane_of == ORDER - 1).astype(F32).astype(BF16)
    first = jnp.dot(coef, flip, preferred_element_type=F32)[:1]
    lane = lax.broadcasted_iota(jnp.int32, (1, 256), 1)
    first = jnp.where(lane == ORDER, 1.0, -first)
    matrix = pltpu.roll(jnp.broadcast_to(first, (BLOCK, 256)), 0, 1, stride=1, stride_axis=0).astype(BF16)
    mis_matrix = pltpu.roll(jnp.broadcast_to(first, (128, 256)), ORDER, 1, stride=1, stride_axis=0).astype(BF16)

    def whiten_misfit(tail):
        here = mis[...].astype(F32)
        row_of = lax.broadcasted_iota(jnp.int32, (16, 128), 0)
        previous = jnp.where(row_of == 0, pltpu.roll(tail, 1, 0), pltpu.roll(here, 1, 0))
        both = jnp.concatenate([previous, here], axis=1).astype(BF16)
        return lax.dot_general(both, mis_matrix, (((1,), (1,)), ((), ())), preferred_element_type=F32)

    def put_misfit(white_mis, i):
        wm_rows[:, i * 128 : (i + 1) * 128] = jnp.broadcast_to(white_mis[i : i + 1], (16, 128)).astype(BF16)

    white_mis = whiten_misfit(jnp.zeros((16, 128), F32))
    for i in range(1, 16):
        put_misfit(white_mis, i)

    def whiten(start, rows):
        out = jnp.dot(
            matrix[:rows, : rows + ORDER], xbuf[start : start + rows + ORDER], preferred_element_type=F32
        )
        white[start : start + rows] = out.astype(BF16)

    def transpose(i):
        white_t[:, i * KROWS : (i + 1) * KROWS] = white[i * KROWS : (i + 1) * KROWS].T

    ready, turned = CHUNKS, ROWS // KROWS
    for start in list(range(0, ROWS, BLOCK))[:0:-1]:
        rows = min(BLOCK, ROWS - start)
        while ready * step_rows > start - ORDER:
            ready -= 1
            loads[ready].wait()
        whiten(start, rows)
        while (turned - 1) * KROWS >= start:
            turned -= 1
            transpose(turned)
    while ready > 0:
        ready -= 1
        loads[ready].wait()

    pl.semaphore_wait(barrier, len(partners))

    halo = pltpu.make_async_remote_copy(
        src_ref=jac.at[pl.ds(ROWS - ORDER, ORDER)], dst_ref=xbuf.at[pl.ds(0, ORDER)],
        send_sem=halo_ss.at[0], recv_sem=halo_rs.at[0], device_id={"tm": after}, device_id_type=MESH,
    )
    mis_halo = pltpu.make_async_remote_copy(
        src_ref=mis, dst_ref=mis_tail,
        send_sem=halo_ss.at[1], recv_sem=halo_rs.at[1], device_id={"tm": after}, device_id_type=MESH,
    )

    @pl.when(me < OWNERS - 1)
    def _():
        halo.start()
        mis_halo.start()

    def gram_a(low, high):
        lhs = jnp.concatenate([white_t[:, low:high], wm_rows[:, low:high]], axis=0)
        return jnp.dot(lhs, white[low:high, :ACOLS], preferred_element_type=F32)

    def gram_b(xo, low, high):
        lhs = white_t[pl.ds(pl.multiple_of(xo * 256, 256), 256), low:high]
        lhs = jnp.concatenate([lhs, wm_rows[:, low:high]], axis=0)
        return jnp.dot(lhs, white[low:high, ACOLS:], preferred_element_type=F32)

    x_order = [2, 1, 3, 0]
    x_of = [lax.rem(x + dx, NX) for dx in x_order]

    acc_a[...] = gram_a(KROWS, ROWS)
    acc_b[0] = gram_b(x_of[0], KROWS, ROWS)

    @pl.when(me > 0)
    def _():
        halo.wait_recv()
        mis_halo.wait_recv()

    @pl.when(me == 0)
    def _():
        xbuf[:ORDER] = jnp.zeros((ORDER, WIDTH), BF16)
        mis_tail[...] = jnp.zeros_like(mis_tail)

    whiten(0, BLOCK)
    transpose(0)
    put_misfit(whiten_misfit(mis_tail[...].astype(F32)), 0)

    def to_sibling(src, dst, k):
        return pltpu.make_async_remote_copy(
            src_ref=src, dst_ref=dst, send_sem=core_ss.at[k], recv_sem=core_rs.at[k],
            device_id={"tm": sibling}, device_id_type=MESH,
        )

    def deal(take, row, keep, send, index):
        keep[index] = folded(take(row + 8 * c))
        send[index] = folded(take(row + 8 - 8 * c)).astype(BF16)

    def eight(row):
        return pl.ds(pl.multiple_of(row, 8), 8)

    acc_a[...] += gram_a(0, KROWS)
    terms = [two_terms(acc_a[WIDTH : WIDTH + 8, t * 128 : t * 128 + 128]) for t in range(2)]
    for own in range(NZ * NY * NC):
        t = own // 16
        at = (slice(own * 8, own * 8 + 8), slice(t * 128, t * 128 + 128))
        acc_a[at] = place(acc_a[at], own % 16 * 8, *terms[t])
    for xo in range(NX):
        for zo in range(NZ):
            for yo in range(NY):
                row = xo * 256 + (zo * NY + yo) * NC * 8
                deal(lambda row: acc_a[eight(row)], row, keep_a, core_sa, zo * NU + xo * NY + yo)
    core_a = to_sibling(core_sa, core_ra, 0)
    core_a.start()

    stage1a, stage1b, core_b = [], [], []

    def tile_of(xo, high):
        return jnp.maximum(xo * 2 + high - 2, 0), jnp.where(xo > 0, 0, 4096)

    def finish_b(step):
        xo = x_of[step]
        for high in range(2):
            tile, off = tile_of(xo, high)
            lanes = pl.ds(pl.multiple_of(tile * 128, 128), 128)
            high_term, low_term = two_terms(acc_b[step, 256:264, lanes])
            for own in range(16):
                row = high * 128 + own * 8
                acc_b[step, row : row + 8, lanes] = place(
                    acc_b[step, row : row + 8, lanes], own * 8 + off, high_term, low_term
                )
        for zo in range(NZ):
            for yo in range(NY):
                deal(
                    lambda row: acc_b[step, eight(row)], (zo * NY + yo) * NC * 8,
                    keep_b, core_sb, (xo * NY + yo) * NZ + zo,
                )
        span = pl.ds(xo * 16, 16)
        copy = to_sibling(core_sb.at[span], core_rb.at[span], 1 + step)
        copy.start()
        core_b.append(copy)

    def again_b(ref, index, xo, high, base):
        tile, off = tile_of(xo, high)
        at = (index, eight(tile // 3 * 8), pl.ds(pl.multiple_of(tile % 3 * 128, 128), 128))
        ref[at] = split_again(ref[at], base + off)

    def send_a():
        core_a.wait_recv()
        keep_a[...] += core_ra[...].astype(F32)
        for zo in range(NZ):
            for yo in range(NY):
                at = (zo * NU + yo, slice(zo // 4 * 8, zo // 4 * 8 + 8))
                keep_a[at] = split_again(keep_a[at], (zo % 4 * 4 + yo * NC + c) * 8)
        s1a[...] = keep_a[...].astype(BF16)
        for k, (device, own) in enumerate(zip(z_dev, z_own)):
            copy = pltpu.make_async_remote_copy(
                src_ref=s1a.at[pl.ds(own * NU, NU)], dst_ref=r1a.at[k],
                send_sem=s1a_ss.at[k], recv_sem=s1a_rs.at[k], device_id={"tm": device}, device_id_type=MESH,
            )
            copy.start()
            stage1a.append(copy)

    def send_b(step):
        xo = x_of[step]
        core_b[step].wait_recv()
        span = pl.ds(xo * 16, 16)
        keep_b[span] += core_rb[span].astype(F32)
        for yo in range(NY):
            for zo in range(NZ):
                again_b(keep_b, (xo * NY + yo) * NZ + zo, xo, zo // 4, (zo % 4 * 4 + yo * NC + c) * 8)
        s1b[span] = keep_b[span].astype(BF16)
        for k, (device, own) in enumerate(zip(xy_dev, xy_own)):
            if XY_STEPS[k][0] == x_order[step]:
                copy = pltpu.make_async_remote_copy(
                    src_ref=s1b.at[pl.ds(own * NZ, NZ)], dst_ref=r1b.at[k],
                    send_sem=s1b_ss.at[k], recv_sem=s1b_rs.at[k], device_id={"tm": device}, device_id_type=MESH,
                )
                copy.start()
                stage1b.append((k, copy))

    acc_b[0] += gram_b(x_of[0], 0, KROWS)
    finish_b(0)
    for step in range(1, NX):
        acc_b[step] = gram_b(x_of[step], 0, ROWS)
        finish_b(step)
        if step == 1:
            send_a()
        send_b(step - 1)
    send_b(NX - 1)

    a2[...] = keep_a[pl.ds(z * NU, NU)]
    for k, copy in enumerate(stage1a):
        copy.wait_recv()
        a2[...] += r1a[k].astype(F32)
    for yo in range(NY):
        at = (yo, eight(z // 4 * 8))
        a2[at] = split_again(a2[at], (z % 4 * 4 + yo * NC + c) * 8)
    s2a[...] = a2[...].astype(BF16)
    stage2a = []
    for k, (device, own) in enumerate(zip(xy_dev, xy_own)):
        copy = pltpu.make_async_remote_copy(
            src_ref=s2a.at[own], dst_ref=r2a.at[k],
            send_sem=s2a_ss.at[k], recv_sem=s2a_rs.at[k], device_id={"tm": device}, device_id_type=MESH,
        )
        copy.start()
        stage2a.append(copy)

    b2[...] = keep_b[pl.ds(u * NZ, NZ)]
    for k, copy in stage1b:
        copy.wait_recv()
        b2[...] += r1b[k].astype(F32)
    for zo in range(NZ):
        again_b(b2, zo, x, zo // 4, (zo % 4 * 4 + y * NC + c) * 8)
    s2b[...] = b2[...].astype(BF16)
    stage2b = []
    for k, (device, own) in enumerate(zip(z_dev, z_own)):
        copy = pltpu.make_async_remote_copy(
            src_ref=s2b.at[own], dst_ref=r2b.at[k],
            send_sem=s2b_ss.at[k], recv_sem=s2b_rs.at[k], device_id={"tm": device}, device_id_type=MESH,
        )
        copy.start()
        stage2b.append(copy)

    last_a, last_b = a2[u], b2[z]
    for k, copy in enumerate(stage2a):
        copy.wait_recv()
        last_a = last_a + r2a[k].astype(F32)

    @pl.when(me < OWNERS - 1)
    def _():
        halo.wait_send()
        mis_halo.wait_send()

    for copy in [core_a] + core_b + stage1a + [copy for _, copy in stage1b] + stage2a:
        copy.wait_send()

    for k, copy in enumerate(stage2b):
        copy.wait_recv()
        last_b = last_b + r2b[k].astype(F32)
    rows_out[:, :ACOLS] = unfolded(last_a)
    rows_out[:, ACOLS:] = unfolded(last_b)

    for copy in stage2b:
        copy.wait_send()


def outputs(rows_ref, fisher, newton):
    rows = rows_ref[...]
    r = lax.broadcasted_iota(jnp.int32, rows.shape, 0)
    col = lax.broadcasted_iota(jnp.int32, rows.shape, 1) - lax.axis_index("tm") * 8
    one, two, on = col == lax.rem(r + 1, 8), col == lax.rem(r + 2, 8), col == r

    def picked(mask, values):
        return jnp.broadcast_to(jnp.sum(jnp.where(mask, values, 0.0), axis=1, keepdims=True), (8, 128))

    grad = pltpu.roll(picked(one, rows), 1, 0) + pltpu.roll(picked(two, rows), 2, 0)
    diagonal = picked(on, rows)
    mirror_one = picked(on, pltpu.roll(rows, 7, 0))[:, :1]
    mirror_two = picked(on, pltpu.roll(rows, 6, 0))[:, :1]
    fisher[...] = jnp.where(one, mirror_one, jnp.where(two, mirror_two, rows)) * (1.0 / TOTAL)
    r8 = lax.broadcasted_iota(jnp.int32, (8, 128), 0)
    c8 = lax.broadcasted_iota(jnp.int32, (8, 128), 1)
    newton[...] = jnp.sum(jnp.where(r8 == c8, grad / diagonal, 0.0), axis=0, keepdims=True)[:, :8]


def shards(jacobian, misfit, taps):
    dma = pltpu.SemaphoreType.DMA
    vmem = pl.BlockSpec(memory_space=pltpu.VMEM)
    rows = pl.pallas_call(
        kernel,
        out_shape=jax.ShapeDtypeStruct((8, WIDTH), F32),
        in_specs=[pl.BlockSpec(memory_space=pl.ANY), vmem, vmem],
        out_specs=vmem,
        scratch_shapes=[
            pltpu.VMEM((ROWS + ORDER, WIDTH), BF16),
            pltpu.VMEM((ROWS, WIDTH), BF16),
            pltpu.VMEM((WIDTH, ROWS), BF16),
            pltpu.VMEM((16, ROWS), BF16),
            pltpu.VMEM((16, 128), BF16),
            pltpu.VMEM((WIDTH + 16, ACOLS), F32),
            pltpu.VMEM((NX, 256 + 16, BCOLS), F32),
            pltpu.VMEM((64, 16, AHALF), F32),
            pltpu.VMEM((64, 16, BHALF), F32),
            pltpu.VMEM((64, 16, AHALF), BF16),
            pltpu.VMEM((64, 16, BHALF), BF16),
            pltpu.VMEM((64, 16, AHALF), BF16),
            pltpu.VMEM((64, 16, BHALF), BF16),
            pltpu.VMEM((64, 16, AHALF), BF16),
            pltpu.VMEM((64, 16, BHALF), BF16),
            pltpu.VMEM((7, 8, 16, AHALF), BF16),
            pltpu.VMEM((7, 8, 16, BHALF), BF16),
            pltpu.VMEM((8, 16, AHALF), F32),
            pltpu.VMEM((8, 16, BHALF), F32),
            pltpu.VMEM((8, 16, AHALF), BF16),
            pltpu.VMEM((8, 16, BHALF), BF16),
            pltpu.VMEM((7, 16, AHALF), BF16),
            pltpu.VMEM((7, 16, BHALF), BF16),
            dma((CHUNKS,)), dma((2,)), dma((2,)), dma((5,)), dma((5,)),
            dma((7,)), dma((7,)), dma((7,)), dma((7,)), dma((7,)), dma((7,)), dma((7,)), dma((7,)),
        ],
        compiler_params=pltpu.CompilerParams(
            collective_id=0, has_side_effects=True, vmem_limit_bytes=56 * 1024 * 1024
        ),
    )(jacobian, misfit.reshape(16, 128), taps.reshape(1, ORDER))
    fisher, newton = pl.pallas_call(
        outputs,
        out_shape=(jax.ShapeDtypeStruct((8, WIDTH), F32), jax.ShapeDtypeStruct((1, 8), F32)),
        in_specs=[vmem],
        out_specs=(vmem, vmem),
    )(rows)
    return fisher, newton.reshape(8)


def solution(mesh):
    in_specs = (P(("net", "tm"), None), P(("net", "tm")), P("net"))
    out_specs = (P(("net", "tm"), None), P(("net", "tm")))
    return jax.shard_map(shards, mesh=mesh, in_specs=in_specs, out_specs=out_specs, check_vma=False)
```

time: 43.2 us -> 40.9 us (0.947)
  local copies, waits for them, and re-layouts: 2.55 us -> 0 us
    unnamed x2 -> x0, local copies, waits for them, and re-layouts: 2.55 us -> none
    pallas_call x1 -> x2, Pallas kernels: 39.8 us -> 40.1 us  [the longest x1 38.6 us: shards(): pl.pallas_call(kernel, out_shape=jax.ShapeDtypeStruct((8, WIDTH), F32), i...]
where the time goes in v2:
time: 40.9 us; the launch traced here: 40.7 us
  Pallas kernels  40.1 us (98%)
  between operations  0.64 us (2%)
    pallas_call x1, Pallas kernels, shards(): pl.pallas_call(kernel, out_shape=jax.ShapeDtypeStruct((8, WIDTH), F32), i...  38.6 us
    pallas_call x1, Pallas kernels, shards(): pl.pallas_call(outputs, out_shape=(jax.ShapeDtypeStruct((8, WIDTH), F32),...  1.48 us

profile of v2, /device:TPU:1, one launch (start us, length us, event | category | flops | bytes accessed | tf_op | source)
XLA Modules:
  0.0 40.7 jit_solution(12989002424069329889)
XLA Ops:
  0.6 38.6 %shard_map.50.rows_ref = f32[8,1024]{1,0:T(8,128)} custom-call(bf16[2048,1024]{1,0:T(8,128)(2,1)} %jac.1, bf16[16,128]{1,0:T(8,128)(2,1)} %bitcast.3, f32[1,64]{1,0:T(1,128)} %bitcast.4), custom_call_target="tpu_custom_call" | custom-call | tf_op jit(solution)/shard_map/pallas_call | solution.py:369
  39.2 1.5 %shard_map.51 = (f32[8,1024]{1,0:T(8,128)}, f32[1,8]{1,0:T(1,128)}) custom-call(f32[8,1024]{1,0:T(8,128)} %shard_map.50.rows_ref), custom_call_target="tpu_custom_call" | custom-call | tf_op jit(solution)/shard_map/pallas_call | solution.py:405

commit v3 on v2

v3 whole, which is shorter than its diff:
```python
import jax
import jax.numpy as jnp
from jax import lax
from jax.experimental import pallas as pl
from jax.experimental.pallas import tpu as pltpu
from jax.sharding import PartitionSpec as P

NX, NZ, NY, NC = 4, 8, 2, 2
NU = NX * NY
OWNERS = NX * NZ * NY * NC
MESH = pl.DeviceIdType.MESH
BF16, F32 = jnp.bfloat16, jnp.float32

ROWS, WIDTH, ORDER = 2048, 1024, 64
BLOCK = 192
GREET = 4
CHUNKS = 8
KROWS = 256
ACOLS = 256
BCOLS = WIDTH - ACOLS
AHALF, BHALF = ACOLS // 2, BCOLS // 2
TOTAL = ROWS * OWNERS
XY_STEPS = [(2, 0), (2, 1), (1, 0), (3, 0), (1, 1), (3, 1), (0, 1)]
Z_STEPS = [4, 3, 5, 2, 6, 1, 7]
HALVES, NP = 2, NZ // 2


def position(x, z, y, c):
    return ((lax.rem(x, NX) * NZ + lax.rem(z, NZ)) * NY + lax.rem(y, NY)) * NC + lax.rem(c, NC)


def folded(rows):
    half = rows.shape[1] // 2
    return jnp.concatenate([rows[:, :half], rows[:, half:]], axis=0)


def unfolded(piece):
    return jnp.concatenate([piece[:8], piece[8:]], axis=1)


def place_of(step):
    return (step - 2) % NZ


def beside(shape, base):
    r = lax.broadcasted_iota(jnp.int32, shape, 0)
    lane = lax.broadcasted_iota(jnp.int32, shape, 1) - base
    return lane == lax.rem(r + 1, 8), lane == lax.rem(r + 2, 8)


def two_terms(value):
    high = value.astype(BF16).astype(F32)
    return high, value - high


def place(rows, base, grad):
    one, two = beside(rows.shape, base)
    high, low = two_terms(grad)
    return jnp.where(one, high, jnp.where(two, low, rows))


def split_again(rows, base):
    one, two = beside(rows.shape, base)
    high, low = two_terms(jnp.sum(jnp.where(one | two, rows, 0.0), axis=0, keepdims=True))
    return jnp.where(one, high, jnp.where(two, low, rows))


def in_tiles(rows, first, change):
    if first < 0 or first * 128 >= rows.shape[1]:
        return rows
    low, high = first * 128, first * 128 + 256
    parts = [rows[:, :low], change(rows[:, low:high]), rows[:, high:]]
    return jnp.concatenate([part for part in parts if part.shape[1]], axis=1)


def kernel(
    jac, mis, taps, rows_out,
    xbuf, white, white_t, wm_rows, mis_tail, acc,
    keep_a, keep_b, core_sa, core_sb, core_ra, core_rb,
    s1a, s1b, r1a, r1b, a2, b2, s2a, s2b, r2a, r2b,
    load_sem, halo_ss, halo_rs, core_ss, core_rs,
    s1a_ss, s1a_rs, s1b_ss, s1b_rs, s2a_ss, s2a_rs, s2b_ss, s2b_rs,
):
    me = lax.axis_index("tm")
    x, z, y, c = me // (NZ * NY * NC), (me // (NY * NC)) % NZ, (me // NC) % NY, me % NC
    sibling = position(x, z, y, c + 1)
    after, before = lax.rem(me + 1, OWNERS), lax.rem(me + OWNERS - 1, OWNERS)
    xy_dev = [position(x + dx, z, y + dy, c) for dx, dy in XY_STEPS]
    xy_own = [lax.rem(x + dx, NX) * NY + lax.rem(y + dy, NY) for dx, dy in XY_STEPS]
    z_dev = [position(x, z + dz, y, c) for dz in Z_STEPS]
    z_own = [lax.rem(z + dz, NZ) for dz in Z_STEPS]
    u = x * NY + y
    z_place = [lax.rem(zo + 2 * NZ - z - 2, NZ) for zo in range(NZ)]
    z_rows = [p // NP * 512 + p % NP * 32 for p in z_place]
    z_at = [lax.rem(z + 2 + p, NZ) for p in range(NZ)]

    step_rows = ROWS // CHUNKS
    loads = []
    for i in reversed(range(CHUNKS)):
        load = pltpu.make_async_copy(
            jac.at[pl.ds(i * step_rows, step_rows)],
            xbuf.at[pl.ds(ORDER + i * step_rows, step_rows)],
            load_sem.at[i],
        )
        load.start()
        loads.append(load)
    loads = loads[::-1]

    barrier = pltpu.get_barrier_semaphore()
    partners = [sibling, after, before] + xy_dev + z_dev
    for device in partners:
        pl.semaphore_signal(barrier, inc=1, device_id={"tm": device}, device_id_type=MESH)

    coef = jnp.broadcast_to(taps[...].astype(BF16), (16, ORDER))
    lag_of = lax.broadcasted_iota(jnp.int32, (ORDER, 256), 0)
    lane_of = lax.broadcasted_iota(jnp.int32, (ORDER, 256), 1)
    flip = (lag_of + lane_of == ORDER - 1).astype(F32).astype(BF16)
    first = jnp.dot(coef, flip, preferred_element_type=F32)[:1]
    lane = lax.broadcasted_iota(jnp.int32, (1, 256), 1)
    first = jnp.where(lane == ORDER, 1.0, -first)
    matrix = pltpu.roll(jnp.broadcast_to(first, (BLOCK, 256)), 0, 1, stride=1, stride_axis=0).astype(BF16)
    mis_matrix = pltpu.roll(jnp.broadcast_to(first, (128, 256)), ORDER, 1, stride=1, stride_axis=0).astype(BF16)

    def whiten_misfit(tail):
        here = mis[...].astype(F32)
        row_of = lax.broadcasted_iota(jnp.int32, (16, 128), 0)
        previous = jnp.where(row_of == 0, pltpu.roll(tail, 1, 0), pltpu.roll(here, 1, 0))
        both = jnp.concatenate([previous, here], axis=1).astype(BF16)
        return lax.dot_general(both, mis_matrix, (((1,), (1,)), ((), ())), preferred_element_type=F32)

    def put_misfit(white_mis, i):
        wm_rows[:, i * 128 : (i + 1) * 128] = jnp.broadcast_to(white_mis[i : i + 1], (16, 128)).astype(BF16)

    white_mis = whiten_misfit(jnp.zeros((16, 128), F32))
    for i in range(1, 16):
        put_misfit(white_mis, i)

    def whiten(start, rows):
        out = jnp.dot(
            matrix[:rows, : rows + ORDER], xbuf[start : start + rows + ORDER], preferred_element_type=F32
        )
        white[start : start + rows] = out.astype(BF16)

    def transpose(i):
        block = white[i * KROWS : (i + 1) * KROWS].T
        for zo in range(NZ):
            for xo in range(NX):
                rows = pl.ds(pl.multiple_of(z_rows[zo] + xo * 128, 32), 32)
                white_t[rows, i * KROWS : (i + 1) * KROWS] = block[xo * 256 + zo * 32 : xo * 256 + zo * 32 + 32]

    halo = pltpu.make_async_remote_copy(
        src_ref=jac.at[pl.ds(ROWS - ORDER, ORDER)], dst_ref=xbuf.at[pl.ds(0, ORDER)],
        send_sem=halo_ss.at[0], recv_sem=halo_rs.at[0], device_id={"tm": after}, device_id_type=MESH,
    )
    mis_halo = pltpu.make_async_remote_copy(
        src_ref=mis, dst_ref=mis_tail,
        send_sem=halo_ss.at[1], recv_sem=halo_rs.at[1], device_id={"tm": after}, device_id_type=MESH,
    )

    ready, turned = CHUNKS, ROWS // KROWS
    for start in list(range(0, ROWS, BLOCK))[:0:-1]:
        rows = min(BLOCK, ROWS - start)
        while ready * step_rows > start - ORDER:
            ready -= 1
            loads[ready].wait()
        if start == GREET * BLOCK:
            pl.semaphore_wait(barrier, len(partners))

            @pl.when(me < OWNERS - 1)
            def _():
                halo.start()
                mis_halo.start()

        whiten(start, rows)
        while (turned - 1) * KROWS >= start:
            turned -= 1
            transpose(turned)
    while ready > 0:
        ready -= 1
        loads[ready].wait()

    def gram_a(low, high):
        lhs = jnp.concatenate([white_t[:, low:high], wm_rows[:, low:high]], axis=0)
        return jnp.dot(lhs, white[low:high, :ACOLS], preferred_element_type=F32)

    def gram_b(half, low, high):
        lhs = white_t[half * 512 : half * 512 + 512, low:high]
        lhs = jnp.concatenate([lhs, wm_rows[:, low:high]], axis=0)
        return jnp.dot(lhs, white[low:high, ACOLS:], preferred_element_type=F32)

    acc[...] = gram_b(0, KROWS, ROWS)

    @pl.when(me > 0)
    def _():
        halo.wait_recv()
        mis_halo.wait_recv()

    @pl.when(me == 0)
    def _():
        xbuf[:ORDER] = jnp.zeros((ORDER, WIDTH), BF16)
        mis_tail[...] = jnp.zeros_like(mis_tail)

    whiten(0, BLOCK)
    transpose(0)
    put_misfit(whiten_misfit(mis_tail[...].astype(F32)), 0)

    def to_sibling(src, dst, k):
        return pltpu.make_async_remote_copy(
            src_ref=src, dst_ref=dst, send_sem=core_ss.at[k], recv_sem=core_rs.at[k],
            device_id={"tm": sibling}, device_id_type=MESH,
        )

    mine_first = c == 0

    def base_of(p, yo, side):
        return z_at[p] * 32 + (yo * NC + side) * 8

    def deal(rows, grad, first, p, yo, keep, send, index):
        pair = []
        for side in range(NC):
            part = rows[side * 8 : side * 8 + 8]

            def change(tiles, side=side):
                return place(tiles, base_of(p, yo, side), grad[:, first * 128 : first * 128 + 256])

            pair.append(folded(in_tiles(part, first, change)))
        keep[index] = jnp.where(mine_first, pair[0], pair[1])
        send[index] = jnp.where(mine_first, pair[1], pair[0]).astype(BF16)

    def both_cores(keep, received, index, first, p, yo):
        rows = keep[index] + received[index].astype(F32)
        if first < 0 or first * 128 >= 2 * rows.shape[1]:
            return rows.astype(BF16)
        rows = in_tiles(unfolded(rows), first, lambda tiles: split_again(tiles, base_of(p, yo, c)))
        return folded(rows).astype(BF16)

    stage1a, stage1b, core_b = [], [], []

    def finish_b(half, out):
        for xo in range(NX):
            for pp in range(NP):
                for yo in range(NY):
                    row = xo * 128 + pp * 32 + yo * 16
                    deal(
                        out[row : row + 16], out[512:513], xo * 2 - 2, half * NP + pp, yo,
                        keep_b, core_sb, (half * NU + xo * NY + yo) * NP + pp,
                    )
        span = pl.ds(half * NU * NP, NU * NP)
        copy = to_sibling(core_sb.at[span], core_rb.at[span], 1 + half)
        copy.start()
        core_b.append(copy)

    def send_b(half):
        core_b[half].wait_recv()
        for xo in range(NX):
            for yo in range(NY):
                for pp in range(NP):
                    index = (half * NU + xo * NY + yo) * NP + pp
                    s1b[index] = both_cores(keep_b, core_rb, index, xo * 2 - 2, half * NP + pp, yo)
        for k, (device, own) in enumerate(zip(xy_dev, xy_own)):
            copy = pltpu.make_async_remote_copy(
                src_ref=s1b.at[pl.ds((half * NU + own) * NP, NP)], dst_ref=r1b.at[half, k],
                send_sem=s1b_ss.at[half * 7 + k], recv_sem=s1b_rs.at[half * 7 + k],
                device_id={"tm": device}, device_id_type=MESH,
            )
            copy.start()
            stage1b.append(copy)

    finish_b(0, acc[...] + gram_b(0, 0, KROWS))

    out = gram_a(0, ROWS)
    for half in range(HALVES):
        for xo in range(NX):
            for pp in range(NP):
                for yo in range(NY):
                    row = half * 512 + xo * 128 + pp * 32 + yo * 16
                    p = half * NP + pp
                    deal(
                        out[row : row + 16], out[WIDTH : WIDTH + 1], xo * 2, p, yo,
                        keep_a, core_sa, p * NU + xo * NY + yo,
                    )
    core_a = to_sibling(core_sa, core_ra, 0)
    core_a.start()
    send_b(0)

    finish_b(1, gram_b(1, 0, ROWS))

    core_a.wait_recv()
    for p in range(NZ):
        for xo in range(NX):
            for yo in range(NY):
                index = p * NU + xo * NY + yo
                s1a[index] = both_cores(keep_a, core_ra, index, xo * 2, p, yo)
    for k, (device, step) in enumerate(zip(z_dev, Z_STEPS)):
        copy = pltpu.make_async_remote_copy(
            src_ref=s1a.at[pl.ds(place_of(step) * NU, NU)], dst_ref=r1a.at[k],
            send_sem=s1a_ss.at[k], recv_sem=s1a_rs.at[k], device_id={"tm": device}, device_id_type=MESH,
        )
        copy.start()
        stage1a.append(copy)
    send_b(1)

    stage2b = {}

    def pass_b(half):
        span = pl.ds((half * NU + u) * NP, NP)
        b2[half] = keep_b[span] + core_rb[span].astype(F32)
        for k in range(7):
            stage1b[half * 7 + k].wait_recv()
            b2[half] += r1b[half, k].astype(F32)
        for pp in range(NP):
            p = half * NP + pp
            lane = x * 256 - ACOLS + base_of(p, y, c)
            s2b[p] = folded(split_again(unfolded(b2[half, pp]), lane)).astype(BF16)
        for k, (device, step) in enumerate(zip(z_dev, Z_STEPS)):
            p = place_of(step)
            if p // NP == half:
                copy = pltpu.make_async_remote_copy(
                    src_ref=s2b.at[p], dst_ref=r2b.at[k],
                    send_sem=s2b_ss.at[k], recv_sem=s2b_rs.at[k], device_id={"tm": device}, device_id_type=MESH,
                )
                copy.start()
                stage2b[k] = copy

    pass_b(0)

    span = pl.ds(place_of(0) * NU, NU)
    a2[...] = keep_a[span] + core_ra[span].astype(F32)
    for k, copy in enumerate(stage1a):
        copy.wait_recv()
        a2[...] += r1a[k].astype(F32)
    for xo in range(NX):
        for yo in range(NY):
            rows = a2[xo * NY + yo]
            if xo == 0:
                rows = folded(split_again(unfolded(rows), base_of(place_of(0), yo, c)))
            s2a[xo * NY + yo] = rows.astype(BF16)
    stage2a = []
    for k, (device, own) in enumerate(zip(xy_dev, xy_own)):
        copy = pltpu.make_async_remote_copy(
            src_ref=s2a.at[own], dst_ref=r2a.at[k],
            send_sem=s2a_ss.at[k], recv_sem=s2a_rs.at[k], device_id={"tm": device}, device_id_type=MESH,
        )
        copy.start()
        stage2a.append(copy)

    pass_b(1)

    last_a, last_b = a2[u], b2[place_of(0) // NP, place_of(0) % NP]
    for k, copy in enumerate(stage2a):
        copy.wait_recv()
        last_a = last_a + r2a[k].astype(F32)

    @pl.when(me < OWNERS - 1)
    def _():
        halo.wait_send()
        mis_halo.wait_send()

    for copy in [core_a] + core_b + stage1a + stage1b + stage2a:
        copy.wait_send()

    for k, copy in stage2b.items():
        copy.wait_recv()
        last_b = last_b + r2b[k].astype(F32)
    rows_out[:, :ACOLS] = unfolded(last_a)
    rows_out[:, ACOLS:] = unfolded(last_b)

    for copy in stage2b.values():
        copy.wait_send()


def outputs(rows_ref, fisher, newton):
    rows = rows_ref[...]
    r = lax.broadcasted_iota(jnp.int32, rows.shape, 0)
    col = lax.broadcasted_iota(jnp.int32, rows.shape, 1) - lax.axis_index("tm") * 8
    one, two, on = col == lax.rem(r + 1, 8), col == lax.rem(r + 2, 8), col == r

    def picked(mask, values):
        return jnp.broadcast_to(jnp.sum(jnp.where(mask, values, 0.0), axis=1, keepdims=True), (8, 128))

    grad = pltpu.roll(picked(one, rows), 1, 0) + pltpu.roll(picked(two, rows), 2, 0)
    diagonal = picked(on, rows)
    mirror_one = picked(on, pltpu.roll(rows, 7, 0))[:, :1]
    mirror_two = picked(on, pltpu.roll(rows, 6, 0))[:, :1]
    fisher[...] = jnp.where(one, mirror_one, jnp.where(two, mirror_two, rows)) * (1.0 / TOTAL)
    r8 = lax.broadcasted_iota(jnp.int32, (8, 128), 0)
    c8 = lax.broadcasted_iota(jnp.int32, (8, 128), 1)
    newton[...] = jnp.sum(jnp.where(r8 == c8, grad / diagonal, 0.0), axis=0, keepdims=True)[:, :8]


def shards(jacobian, misfit, taps):
    dma = pltpu.SemaphoreType.DMA
    vmem = pl.BlockSpec(memory_space=pltpu.VMEM)
    rows = pl.pallas_call(
        kernel,
        out_shape=jax.ShapeDtypeStruct((8, WIDTH), F32),
        in_specs=[pl.BlockSpec(memory_space=pl.ANY), vmem, vmem],
        out_specs=vmem,
        scratch_shapes=[
            pltpu.VMEM((ROWS + ORDER, WIDTH), BF16),
            pltpu.VMEM((ROWS, WIDTH), BF16),
            pltpu.VMEM((WIDTH, ROWS), BF16),
            pltpu.VMEM((16, ROWS), BF16),
            pltpu.VMEM((16, 128), BF16),
            pltpu.VMEM((512 + 16, BCOLS), F32),
            pltpu.VMEM((64, 16, AHALF), F32),
            pltpu.VMEM((64, 16, BHALF), F32),
            pltpu.VMEM((64, 16, AHALF), BF16),
            pltpu.VMEM((64, 16, BHALF), BF16),
            pltpu.VMEM((64, 16, AHALF), BF16),
            pltpu.VMEM((64, 16, BHALF), BF16),
            pltpu.VMEM((64, 16, AHALF), BF16),
            pltpu.VMEM((64, 16, BHALF), BF16),
            pltpu.VMEM((7, 8, 16, AHALF), BF16),
            pltpu.VMEM((HALVES, 7, NP, 16, BHALF), BF16),
            pltpu.VMEM((8, 16, AHALF), F32),
            pltpu.VMEM((HALVES, NP, 16, BHALF), F32),
            pltpu.VMEM((8, 16, AHALF), BF16),
            pltpu.VMEM((8, 16, BHALF), BF16),
            pltpu.VMEM((7, 16, AHALF), BF16),
            pltpu.VMEM((7, 16, BHALF), BF16),
            dma((CHUNKS,)), dma((2,)), dma((2,)), dma((3,)), dma((3,)),
            dma((7,)), dma((7,)), dma((14,)), dma((14,)), dma((7,)), dma((7,)), dma((7,)), dma((7,)),
        ],
        compiler_params=pltpu.CompilerParams(
            collective_id=0, has_side_effects=True, vmem_limit_bytes=56 * 1024 * 1024
        ),
    )(jacobian, misfit.reshape(16, 128), taps.reshape(1, ORDER))
    fisher, newton = pl.pallas_call(
        outputs,
        out_shape=(jax.ShapeDtypeStruct((8, WIDTH), F32), jax.ShapeDtypeStruct((1, 8), F32)),
        in_specs=[vmem],
        out_specs=(vmem, vmem),
    )(rows)
    return fisher, newton.reshape(8)


def solution(mesh):
    in_specs = (P(("net", "tm"), None), P(("net", "tm")), P("net"))
    out_specs = (P(("net", "tm"), None), P(("net", "tm")))
    return jax.shard_map(shards, mesh=mesh, in_specs=in_specs, out_specs=out_specs, check_vma=False)
```

time: 40.9 us -> 37.3 us (0.912)
  Pallas kernels: 40.1 us -> 36.5 us
    pallas_call x1, Pallas kernels: 38.6 us -> 35 us  [shards(): pl.pallas_call(kernel, out_shape=jax.ShapeDtypeStruct((8, WIDTH), F32), i...]
where the time goes in v3:
time: 37.3 us; the launch traced here: 37.1 us
  Pallas kernels  36.5 us (98%)
  between operations  0.64 us (2%)
    pallas_call x1, Pallas kernels, shards(): pl.pallas_call(kernel, out_shape=jax.ShapeDtypeStruct((8, WIDTH), F32), i...  35 us
    pallas_call x1, Pallas kernels, shards(): pl.pallas_call(outputs, out_shape=(jax.ShapeDtypeStruct((8, WIDTH), F32),...  1.48 us

profile of v3, /device:TPU:1, one launch (start us, length us, event | category | flops | bytes accessed | tf_op | source)
XLA Modules:
  0.0 37.1 jit_solution(6952302464224547858)
XLA Ops:
  0.6 35.0 %shard_map.50.rows_ref = f32[8,1024]{1,0:T(8,128)} custom-call(bf16[2048,1024]{1,0:T(8,128)(2,1)} %jac.1, bf16[16,128]{1,0:T(8,128)(2,1)} %bitcast.3, f32[1,64]{1,0:T(1,128)} %bitcast.4), custom_call_target="tpu_custom_call" | custom-call | tf_op jit(solution)/shard_map/pallas_call | solution.py:394
  35.6 1.5 %shard_map.51 = (f32[8,1024]{1,0:T(8,128)}, f32[1,8]{1,0:T(1,128)}) custom-call(f32[8,1024]{1,0:T(8,128)} %shard_map.50.rows_ref), custom_call_target="tpu_custom_call" | custom-call | tf_op jit(solution)/shard_map/pallas_call | solution.py:429

commit v4 on v3

--- a/solution.py
+++ b/solution.py
@@ -13,9 +13,11 @@
 
 ROWS, WIDTH, ORDER = 2048, 1024, 64
 BLOCK = 192
-GREET = 4
-CHUNKS = 8
+GREET = 8
+BOUNDS = [0, 512, 1024, 1536, 2048]
+CHUNKS = len(BOUNDS) - 1
 KROWS = 256
+MROWS = 256
 ACOLS = 256
 BCOLS = WIDTH - ACOLS
 AHALF, BHALF = ACOLS // 2, BCOLS // 2
@@ -94,17 +96,13 @@
     z_rows = [p // NP * 512 + p % NP * 32 for p in z_place]
     z_at = [lax.rem(z + 2 + p, NZ) for p in range(NZ)]
 
-    step_rows = ROWS // CHUNKS
     loads = []
-    for i in reversed(range(CHUNKS)):
-        load = pltpu.make_async_copy(
-            jac.at[pl.ds(i * step_rows, step_rows)],
-            xbuf.at[pl.ds(ORDER + i * step_rows, step_rows)],
-            load_sem.at[i],
-        )
+    for i, (low, high) in enumerate(zip(BOUNDS[:-1], BOUNDS[1:])):
+        loads.append(pltpu.make_async_copy(
+            jac.at[pl.ds(low, high - low)], xbuf.at[pl.ds(ORDER + low, high - low)], load_sem.at[i]
+        ))
+    for load in loads[::-1]:
         load.start()
-        loads.append(load)
-    loads = loads[::-1]
 
     barrier = pltpu.get_barrier_semaphore()
     partners = [sibling, after, before] + xy_dev + z_dev
@@ -160,7 +158,7 @@
     ready, turned = CHUNKS, ROWS // KROWS
     for start in list(range(0, ROWS, BLOCK))[:0:-1]:
         rows = min(BLOCK, ROWS - start)
-        while ready * step_rows > start - ORDER:
+        while BOUNDS[ready] > start - ORDER:
             ready -= 1
             loads[ready].wait()
         if start == GREET * BLOCK:
@@ -179,14 +177,20 @@
         ready -= 1
         loads[ready].wait()
 
+    def product(row, rows, left, right, low, high):
+        parts = []
+        for i in range(row, row + rows, MROWS):
+            lhs = white_t[i : i + MROWS, low:high]
+            if i + MROWS == row + rows:
+                lhs = jnp.concatenate([lhs, wm_rows[:, low:high]], axis=0)
+            parts.append(jnp.dot(lhs, white[low:high, left:right], preferred_element_type=F32))
+        return jnp.concatenate(parts, axis=0)
+
     def gram_a(low, high):
-        lhs = jnp.concatenate([white_t[:, low:high], wm_rows[:, low:high]], axis=0)
-        return jnp.dot(lhs, white[low:high, :ACOLS], preferred_element_type=F32)
+        return product(0, WIDTH, 0, ACOLS, low, high)
 
     def gram_b(half, low, high):
-        lhs = white_t[half * 512 : half * 512 + 512, low:high]
-        lhs = jnp.concatenate([lhs, wm_rows[:, low:high]], axis=0)
-        return jnp.dot(lhs, white[low:high, ACOLS:], preferred_element_type=F32)
+        return product(half * 512, 512, ACOLS, WIDTH, low, high)
 
     acc[...] = gram_b(0, KROWS, ROWS)
 

time: 37.3 us -> 36.3 us (0.973)
  Pallas kernels: 36.5 us -> 35.5 us
    pallas_call x1, Pallas kernels: 35 us -> 34 us  [shards(): pl.pallas_call(kernel, out_shape=jax.ShapeDtypeStruct((8, WIDTH), F32), i...]
where the time goes in v4:
time: 36.3 us; the launch traced here: 36.2 us
  Pallas kernels  35.5 us (98%)
  between operations  0.64 us (2%)
    pallas_call x1, Pallas kernels, shards(): pl.pallas_call(kernel, out_shape=jax.ShapeDtypeStruct((8, WIDTH), F32), i...  34 us
    pallas_call x1, Pallas kernels, shards(): pl.pallas_call(outputs, out_shape=(jax.ShapeDtypeStruct((8, WIDTH), F32),...  1.48 us

profile of v4, /device:TPU:1, one launch (start us, length us, event | category | flops | bytes accessed | tf_op | source)
XLA Modules:
  0.0 36.2 jit_solution(3698923683063376077)
XLA Ops:
  0.6 34.0 %shard_map.50.rows_ref = f32[8,1024]{1,0:T(8,128)} custom-call(bf16[2048,1024]{1,0:T(8,128)(2,1)} %jac.1, bf16[16,128]{1,0:T(8,128)(2,1)} %bitcast.3, f32[1,64]{1,0:T(1,128)} %bitcast.4), custom_call_target="tpu_custom_call" | custom-call | tf_op jit(solution)/shard_map/pallas_call | solution.py:398
  34.7 1.5 %shard_map.51 = (f32[8,1024]{1,0:T(8,128)}, f32[1,8]{1,0:T(1,128)}) custom-call(f32[8,1024]{1,0:T(8,128)} %shard_map.50.rows_ref), custom_call_target="tpu_custom_call" | custom-call | tf_op jit(solution)/shard_map/pallas_call | solution.py:433

commit v5 on v4

--- a/solution.py
+++ b/solution.py
@@ -76,8 +76,8 @@
 
 
 def kernel(
-    jac, mis, taps, rows_out,
-    xbuf, white, white_t, wm_rows, mis_tail, acc,
+    jac, mis_in, taps_in, rows_out,
+    mis, taps, xbuf, white, white_t, wm_rows, mis_tail, acc,
     keep_a, keep_b, core_sa, core_sb, core_ra, core_rb,
     s1a, s1b, r1a, r1b, a2, b2, s2a, s2b, r2a, r2b,
     load_sem, halo_ss, halo_rs, core_ss, core_rs,
@@ -101,13 +101,21 @@
         loads.append(pltpu.make_async_copy(
             jac.at[pl.ds(low, high - low)], xbuf.at[pl.ds(ORDER + low, high - low)], load_sem.at[i]
         ))
-    for load in loads[::-1]:
+
+    small = [
+        pltpu.make_async_copy(taps_in, taps, load_sem.at[CHUNKS]),
+        pltpu.make_async_copy(mis_in, mis, load_sem.at[CHUNKS + 1]),
+    ]
+    for load in small + loads[::-1]:
         load.start()
 
     barrier = pltpu.get_barrier_semaphore()
     partners = [sibling, after, before] + xy_dev + z_dev
     for device in partners:
         pl.semaphore_signal(barrier, inc=1, device_id={"tm": device}, device_id_type=MESH)
+
+    for load in small:
+        load.wait()
 
     coef = jnp.broadcast_to(taps[...].astype(BF16), (16, ORDER))
     lag_of = lax.broadcasted_iota(jnp.int32, (ORDER, 256), 0)
@@ -143,15 +151,15 @@
         block = white[i * KROWS : (i + 1) * KROWS].T
         for zo in range(NZ):
             for xo in range(NX):
-                rows = pl.ds(pl.multiple_of(z_rows[zo] + xo * 128, 32), 32)
-                white_t[rows, i * KROWS : (i + 1) * KROWS] = block[xo * 256 + zo * 32 : xo * 256 + zo * 32 + 32]
+                pass
+        white_t[:, i * KROWS : (i + 1) * KROWS] = block
 
     halo = pltpu.make_async_remote_copy(
         src_ref=jac.at[pl.ds(ROWS - ORDER, ORDER)], dst_ref=xbuf.at[pl.ds(0, ORDER)],
         send_sem=halo_ss.at[0], recv_sem=halo_rs.at[0], device_id={"tm": after}, device_id_type=MESH,
     )
     mis_halo = pltpu.make_async_remote_copy(
-        src_ref=mis, dst_ref=mis_tail,
+        src_ref=mis_in, dst_ref=mis_tail,
         send_sem=halo_ss.at[1], recv_sem=halo_rs.at[1], device_id={"tm": after}, device_id_type=MESH,
     )
 
@@ -177,10 +185,16 @@
         ready -= 1
         loads[ready].wait()
 
+    def z_group(row):
+        half, xo, pp = row // 512, row // 128 % NX, row // 32 % NP
+        return pl.ds(pl.multiple_of(xo * 256 + z_at[half * NP + pp] * 32, 32), 32)
+
     def product(row, rows, left, right, low, high):
         parts = []
         for i in range(row, row + rows, MROWS):
-            lhs = white_t[i : i + MROWS, low:high]
+            lhs = jnp.concatenate(
+                [white_t[z_group(j), low:high] for j in range(i, i + MROWS, 32)], axis=0
+            )
             if i + MROWS == row + rows:
                 lhs = jnp.concatenate([lhs, wm_rows[:, low:high]], axis=0)
             parts.append(jnp.dot(lhs, white[low:high, left:right], preferred_element_type=F32))
@@ -397,10 +411,12 @@
     vmem = pl.BlockSpec(memory_space=pltpu.VMEM)
     rows = pl.pallas_call(
         kernel,
-        out_shape=jax.ShapeDtypeStruct((8, WIDTH), F32),
-        in_specs=[pl.BlockSpec(memory_space=pl.ANY), vmem, vmem],
+        out_shape=pltpu.VMEM((8, WIDTH), F32),
+        in_specs=[pl.BlockSpec(memory_space=pl.ANY)] * 3,
         out_specs=vmem,
         scratch_shapes=[
+            pltpu.VMEM((16, 128), BF16),
+            pltpu.VMEM((1, ORDER), F32),
             pltpu.VMEM((ROWS + ORDER, WIDTH), BF16),
             pltpu.VMEM((ROWS, WIDTH), BF16),
             pltpu.VMEM((WIDTH, ROWS), BF16),
@@ -423,7 +439,7 @@
             pltpu.VMEM((8, 16, BHALF), BF16),
             pltpu.VMEM((7, 16, AHALF), BF16),
             pltpu.VMEM((7, 16, BHALF), BF16),
-            dma((CHUNKS,)), dma((2,)), dma((2,)), dma((3,)), dma((3,)),
+            dma((CHUNKS + 2,)), dma((2,)), dma((2,)), dma((3,)), dma((3,)),
             dma((7,)), dma((7,)), dma((14,)), dma((14,)), dma((7,)), dma((7,)), dma((7,)), dma((7,)),
         ],
         compiler_params=pltpu.CompilerParams(
@@ -435,7 +451,7 @@
         out_shape=(jax.ShapeDtypeStruct((8, WIDTH), F32), jax.ShapeDtypeStruct((1, 8), F32)),
         in_specs=[vmem],
         out_specs=(vmem, vmem),
-    )(rows)
+    )(pltpu.with_memory_space_constraint(rows, pltpu.VMEM))
     return fisher, newton.reshape(8)
 
 

time: 36.3 us -> 34.3 us (0.945)
  Pallas kernels: 35.5 us -> 33.6 us
    pallas_call x1, Pallas kernels: 34 us -> 32.9 us  [shards(): pl.pallas_call(kernel, out_shape=pltpu.VMEM((8, WIDTH), F32), in_specs=[p...]
    pallas_call x1, Pallas kernels: 1.48 us -> 0.72 us  [shards(): pl.pallas_call(outputs, out_shape=(jax.ShapeDtypeStruct((8, WIDTH), F32),...]
where the time goes in v5:
time: 34.3 us; the launch traced here: 34.2 us
  Pallas kernels  33.6 us (98%)
  between operations  0.64 us (2%)
    pallas_call x1, Pallas kernels, shards(): pl.pallas_call(kernel, out_shape=pltpu.VMEM((8, WIDTH), F32), in_specs=[p...  32.9 us
    pallas_call x1, Pallas kernels, shards(): pl.pallas_call(outputs, out_shape=(jax.ShapeDtypeStruct((8, WIDTH), F32),...  0.72 us

profile of v5, /device:TPU:1, one launch (start us, length us, event | category | flops | bytes accessed | tf_op | source)
XLA Modules:
  0.0 34.2 jit_solution(6498763364762171194)
XLA Ops:
  0.6 32.9 %shard_map.50.rows_ref = f32[8,1024]{1,0:T(8,128)S(1)} custom-call(bf16[2048,1024]{1,0:T(8,128)(2,1)} %jac.1, bf16[16,128]{1,0:T(8,128)(2,1)} %bitcast.3, f32[1,64]{1,0:T(1,128)} %bitcast.4), custom_call_target="tpu_custom_call" | custom-call | tf_op jit(solution)/shard_map/pallas_call | solution.py:412
  33.5 0.7 %shard_map.51 = (f32[8,1024]{1,0:T(8,128)}, f32[1,8]{1,0:T(1,128)}) custom-call(f32[8,1024]{1,0:T(8,128)S(1)} %shard_map.50.rows_ref), custom_call_target="tpu_custom_call" | custom-call | tf_op jit(solution)/shard_map/pallas_call | solution.py:449

commit v6 on v5

--- a/solution.py
+++ b/solution.py
@@ -22,7 +22,7 @@
 BCOLS = WIDTH - ACOLS
 AHALF, BHALF = ACOLS // 2, BCOLS // 2
 TOTAL = ROWS * OWNERS
-XY_STEPS = [(2, 0), (2, 1), (1, 0), (3, 0), (1, 1), (3, 1), (0, 1)]
+XY_STEPS = [(0, 1), (2, 1), (1, 1), (3, 1), (2, 0), (1, 0), (3, 0)]
 Z_STEPS = [4, 3, 5, 2, 6, 1, 7]
 HALVES, NP = 2, NZ // 2
 

time: 34.3 us -> 33.6 us (0.980)
  Pallas kernels: 33.6 us -> 32.9 us
    pallas_call x1, Pallas kernels: 32.9 us -> 32.2 us  [shards(): pl.pallas_call(kernel, out_shape=pltpu.VMEM((8, WIDTH), F32), in_specs=[p...]
where the time goes in v6:
time: 33.6 us; the launch traced here: 33.5 us
  Pallas kernels  32.9 us (98%)
  between operations  0.64 us (2%)
    pallas_call x1, Pallas kernels, shards(): pl.pallas_call(kernel, out_shape=pltpu.VMEM((8, WIDTH), F32), in_specs=[p...  32.2 us
    pallas_call x1, Pallas kernels, shards(): pl.pallas_call(outputs, out_shape=(jax.ShapeDtypeStruct((8, WIDTH), F32),...  0.72 us

profile of v6, /device:TPU:1, one launch (start us, length us, event | category | flops | bytes accessed | tf_op | source)
XLA Modules:
  0.0 33.5 jit_solution(8938942903480040222)
XLA Ops:
  0.6 32.2 %shard_map.50.rows_ref = f32[8,1024]{1,0:T(8,128)S(1)} custom-call(bf16[2048,1024]{1,0:T(8,128)(2,1)} %jac.1, bf16[16,128]{1,0:T(8,128)(2,1)} %bitcast.3, f32[1,64]{1,0:T(1,128)} %bitcast.4), custom_call_target="tpu_custom_call" | custom-call | tf_op jit(solution)/shard_map/pallas_call | solution.py:412
  32.8 0.7 %shard_map.51 = (f32[8,1024]{1,0:T(8,128)}, f32[1,8]{1,0:T(1,128)}) custom-call(f32[8,1024]{1,0:T(8,128)S(1)} %shard_map.50.rows_ref), custom_call_target="tpu_custom_call" | custom-call | tf_op jit(solution)/shard_map/pallas_call | solution.py:449

commit v7 on v6

--- a/solution.py
+++ b/solution.py
@@ -24,7 +24,9 @@
 TOTAL = ROWS * OWNERS
 XY_STEPS = [(0, 1), (2, 1), (1, 1), (3, 1), (2, 0), (1, 0), (3, 0)]
 Z_STEPS = [4, 3, 5, 2, 6, 1, 7]
-HALVES, NP = 2, NZ // 2
+GROUPS = [(0, 4), (4, 8)]
+PLAN = [("gram", "a"), ("send", 0), ("send", "a"), ("gram", 1), ("send", 1)]
+PASSES = [0, "a", 1]
 
 
 def position(x, z, y, c):
@@ -92,8 +94,6 @@
     z_dev = [position(x, z + dz, y, c) for dz in Z_STEPS]
     z_own = [lax.rem(z + dz, NZ) for dz in Z_STEPS]
     u = x * NY + y
-    z_place = [lax.rem(zo + 2 * NZ - z - 2, NZ) for zo in range(NZ)]
-    z_rows = [p // NP * 512 + p % NP * 32 for p in z_place]
     z_at = [lax.rem(z + 2 + p, NZ) for p in range(NZ)]
 
     loads = []
@@ -185,26 +185,26 @@
         ready -= 1
         loads[ready].wait()
 
-    def z_group(row):
-        half, xo, pp = row // 512, row // 128 % NX, row // 32 % NP
-        return pl.ds(pl.multiple_of(xo * 256 + z_at[half * NP + pp] * 32, 32), 32)
-
-    def product(row, rows, left, right, low, high):
-        parts = []
-        for i in range(row, row + rows, MROWS):
-            lhs = jnp.concatenate(
-                [white_t[z_group(j), low:high] for j in range(i, i + MROWS, 32)], axis=0
-            )
-            if i + MROWS == row + rows:
-                lhs = jnp.concatenate([lhs, wm_rows[:, low:high]], axis=0)
-            parts.append(jnp.dot(lhs, white[low:high, left:right], preferred_element_type=F32))
+    def z_group(low, high, row):
+        xo, p = row // ((high - low) * 32), low + row // 32 % (high - low)
+        return pl.ds(pl.multiple_of(xo * 256 + z_at[p] * 32, 32), 32)
+
+    def product(group, left, right, first, last):
+        low, high = group
+        rows, parts = NX * (high - low) * 32, []
+        for i in range(0, rows, MROWS):
+            lhs = [white_t[z_group(low, high, j), first:last] for j in range(i, i + MROWS, 32)]
+            if i + MROWS == rows:
+                lhs.append(wm_rows[:, first:last])
+            lhs = jnp.concatenate(lhs, axis=0)
+            parts.append(jnp.dot(lhs, white[first:last, left:right], preferred_element_type=F32))
         return jnp.concatenate(parts, axis=0)
 
-    def gram_a(low, high):
-        return product(0, WIDTH, 0, ACOLS, low, high)
-
-    def gram_b(half, low, high):
-        return product(half * 512, 512, ACOLS, WIDTH, low, high)
+    def gram_a(first, last):
+        return product((0, NZ), 0, ACOLS, first, last)
+
+    def gram_b(g, first, last):
+        return product(GROUPS[g], ACOLS, WIDTH, first, last)
 
     acc[...] = gram_b(0, KROWS, ROWS)
 
@@ -252,87 +252,100 @@
         rows = in_tiles(unfolded(rows), first, lambda tiles: split_again(tiles, base_of(p, yo, c)))
         return folded(rows).astype(BF16)
 
-    stage1a, stage1b, core_b = [], [], []
-
-    def finish_b(half, out):
+    stage1a, stage1b, stage2a, stage2b, core = [], {}, [], {}, {}
+
+    def slot(g, own, p):
+        low, high = GROUPS[g]
+        return low * NU + own * (high - low) + p - low
+
+    def finish_b(g, out):
+        low, high = GROUPS[g]
+        row = 0
         for xo in range(NX):
-            for pp in range(NP):
+            for p in range(low, high):
                 for yo in range(NY):
-                    row = xo * 128 + pp * 32 + yo * 16
                     deal(
-                        out[row : row + 16], out[512:513], xo * 2 - 2, half * NP + pp, yo,
-                        keep_b, core_sb, (half * NU + xo * NY + yo) * NP + pp,
+                        out[row : row + 16], out[-16:-15], xo * 2 - 2, p, yo,
+                        keep_b, core_sb, slot(g, xo * NY + yo, p),
                     )
-        span = pl.ds(half * NU * NP, NU * NP)
-        copy = to_sibling(core_sb.at[span], core_rb.at[span], 1 + half)
-        copy.start()
-        core_b.append(copy)
-
-    def send_b(half):
-        core_b[half].wait_recv()
+                    row += 16
+        span = pl.ds(low * NU, (high - low) * NU)
+        core[g] = to_sibling(core_sb.at[span], core_rb.at[span], 1 + g)
+        core[g].start()
+
+    def send_b(g):
+        low, high = GROUPS[g]
+        core[g].wait_recv()
         for xo in range(NX):
             for yo in range(NY):
-                for pp in range(NP):
-                    index = (half * NU + xo * NY + yo) * NP + pp
-                    s1b[index] = both_cores(keep_b, core_rb, index, xo * 2 - 2, half * NP + pp, yo)
+                for p in range(low, high):
+                    index = slot(g, xo * NY + yo, p)
+                    s1b[index] = both_cores(keep_b, core_rb, index, xo * 2 - 2, p, yo)
         for k, (device, own) in enumerate(zip(xy_dev, xy_own)):
             copy = pltpu.make_async_remote_copy(
-                src_ref=s1b.at[pl.ds((half * NU + own) * NP, NP)], dst_ref=r1b.at[half, k],
-                send_sem=s1b_ss.at[half * 7 + k], recv_sem=s1b_rs.at[half * 7 + k],
+                src_ref=s1b.at[pl.ds(slot(g, own, low), high - low)], dst_ref=r1b.at[k, low:high],
+                send_sem=s1b_ss.at[g * 7 + k], recv_sem=s1b_rs.at[g * 7 + k],
                 device_id={"tm": device}, device_id_type=MESH,
             )
             copy.start()
-            stage1b.append(copy)
-
-    finish_b(0, acc[...] + gram_b(0, 0, KROWS))
-
-    out = gram_a(0, ROWS)
-    for half in range(HALVES):
+            stage1b[g, k] = copy
+
+    def finish_a(out):
+        row = 0
         for xo in range(NX):
-            for pp in range(NP):
+            for p in range(NZ):
                 for yo in range(NY):
-                    row = half * 512 + xo * 128 + pp * 32 + yo * 16
-                    p = half * NP + pp
                     deal(
                         out[row : row + 16], out[WIDTH : WIDTH + 1], xo * 2, p, yo,
                         keep_a, core_sa, p * NU + xo * NY + yo,
                     )
-    core_a = to_sibling(core_sa, core_ra, 0)
-    core_a.start()
-    send_b(0)
-
-    finish_b(1, gram_b(1, 0, ROWS))
-
-    core_a.wait_recv()
-    for p in range(NZ):
-        for xo in range(NX):
-            for yo in range(NY):
-                index = p * NU + xo * NY + yo
-                s1a[index] = both_cores(keep_a, core_ra, index, xo * 2, p, yo)
-    for k, (device, step) in enumerate(zip(z_dev, Z_STEPS)):
-        copy = pltpu.make_async_remote_copy(
-            src_ref=s1a.at[pl.ds(place_of(step) * NU, NU)], dst_ref=r1a.at[k],
-            send_sem=s1a_ss.at[k], recv_sem=s1a_rs.at[k], device_id={"tm": device}, device_id_type=MESH,
-        )
-        copy.start()
-        stage1a.append(copy)
-    send_b(1)
-
-    stage2b = {}
-
-    def pass_b(half):
-        span = pl.ds((half * NU + u) * NP, NP)
-        b2[half] = keep_b[span] + core_rb[span].astype(F32)
+                    row += 16
+        core["a"] = to_sibling(core_sa, core_ra, 0)
+        core["a"].start()
+
+    def send_a():
+        core["a"].wait_recv()
+        for p in range(NZ):
+            for xo in range(NX):
+                for yo in range(NY):
+                    index = p * NU + xo * NY + yo
+                    s1a[index] = both_cores(keep_a, core_ra, index, xo * 2, p, yo)
+        for k, (device, step) in enumerate(zip(z_dev, Z_STEPS)):
+            copy = pltpu.make_async_remote_copy(
+                src_ref=s1a.at[pl.ds(place_of(step) * NU, NU)], dst_ref=r1a.at[k],
+                send_sem=s1a_ss.at[k], recv_sem=s1a_rs.at[k], device_id={"tm": device}, device_id_type=MESH,
+            )
+            copy.start()
+            stage1a.append(copy)
+
+    def send(item):
+        if item == "a":
+            send_a()
+        else:
+            send_b(item)
+
+    finish_b(0, acc[...] + gram_b(0, 0, KROWS))
+    for act, item in PLAN:
+        if act == "send":
+            send(item)
+        elif item == "a":
+            finish_a(gram_a(0, ROWS))
+        else:
+            finish_b(item, gram_b(item, 0, ROWS))
+
+    def pass_b(g):
+        low, high = GROUPS[g]
+        span = pl.ds(slot(g, u, low), high - low)
+        b2[low:high] = keep_b[span] + core_rb[span].astype(F32)
         for k in range(7):
-            stage1b[half * 7 + k].wait_recv()
-            b2[half] += r1b[half, k].astype(F32)
-        for pp in range(NP):
-            p = half * NP + pp
+            stage1b[g, k].wait_recv()
+            b2[low:high] += r1b[k, low:high].astype(F32)
+        for p in range(low, high):
             lane = x * 256 - ACOLS + base_of(p, y, c)
-            s2b[p] = folded(split_again(unfolded(b2[half, pp]), lane)).astype(BF16)
+            s2b[p] = folded(split_again(unfolded(b2[p]), lane)).astype(BF16)
         for k, (device, step) in enumerate(zip(z_dev, Z_STEPS)):
             p = place_of(step)
-            if p // NP == half:
+            if low <= p < high:
                 copy = pltpu.make_async_remote_copy(
                     src_ref=s2b.at[p], dst_ref=r2b.at[k],
                     send_sem=s2b_ss.at[k], recv_sem=s2b_rs.at[k], device_id={"tm": device}, device_id_type=MESH,
@@ -340,31 +353,33 @@
                 copy.start()
                 stage2b[k] = copy
 
-    pass_b(0)
-
-    span = pl.ds(place_of(0) * NU, NU)
-    a2[...] = keep_a[span] + core_ra[span].astype(F32)
-    for k, copy in enumerate(stage1a):
-        copy.wait_recv()
-        a2[...] += r1a[k].astype(F32)
-    for xo in range(NX):
-        for yo in range(NY):
-            rows = a2[xo * NY + yo]
-            if xo == 0:
-                rows = folded(split_again(unfolded(rows), base_of(place_of(0), yo, c)))
-            s2a[xo * NY + yo] = rows.astype(BF16)
-    stage2a = []
-    for k, (device, own) in enumerate(zip(xy_dev, xy_own)):
-        copy = pltpu.make_async_remote_copy(
-            src_ref=s2a.at[own], dst_ref=r2a.at[k],
-            send_sem=s2a_ss.at[k], recv_sem=s2a_rs.at[k], device_id={"tm": device}, device_id_type=MESH,
-        )
-        copy.start()
-        stage2a.append(copy)
-
-    pass_b(1)
-
-    last_a, last_b = a2[u], b2[place_of(0) // NP, place_of(0) % NP]
+    def pass_a():
+        span = pl.ds(place_of(0) * NU, NU)
+        a2[...] = keep_a[span] + core_ra[span].astype(F32)
+        for k, copy in enumerate(stage1a):
+            copy.wait_recv()
+            a2[...] += r1a[k].astype(F32)
+        for xo in range(NX):
+            for yo in range(NY):
+                rows = a2[xo * NY + yo]
+                if xo == 0:
+                    rows = folded(split_again(unfolded(rows), base_of(place_of(0), yo, c)))
+                s2a[xo * NY + yo] = rows.astype(BF16)
+        for k, (device, own) in enumerate(zip(xy_dev, xy_own)):
+            copy = pltpu.make_async_remote_copy(
+                src_ref=s2a.at[own], dst_ref=r2a.at[k],
+                send_sem=s2a_ss.at[k], recv_sem=s2a_rs.at[k], device_id={"tm": device}, device_id_type=MESH,
+            )
+            copy.start()
+            stage2a.append(copy)
+
+    for item in PASSES:
+        if item == "a":
+            pass_a()
+        else:
+            pass_b(item)
+
+    last_a, last_b = a2[u], b2[place_of(0)]
     for k, copy in enumerate(stage2a):
         copy.wait_recv()
         last_a = last_a + r2a[k].astype(F32)
@@ -374,7 +389,7 @@
         halo.wait_send()
         mis_halo.wait_send()
 
-    for copy in [core_a] + core_b + stage1a + stage1b + stage2a:
+    for copy in list(core.values()) + stage1a + list(stage1b.values()) + stage2a:
         copy.wait_send()
 
     for k, copy in stage2b.items():
@@ -422,7 +437,7 @@
             pltpu.VMEM((WIDTH, ROWS), BF16),
             pltpu.VMEM((16, ROWS), BF16),
             pltpu.VMEM((16, 128), BF16),
-            pltpu.VMEM((512 + 16, BCOLS), F32),
+            pltpu.VMEM((NX * (GROUPS[0][1] - GROUPS[0][0]) * 32 + 16, BCOLS), F32),
             pltpu.VMEM((64, 16, AHALF), F32),
             pltpu.VMEM((64, 16, BHALF), F32),
             pltpu.VMEM((64, 16, AHALF), BF16),
@@ -432,15 +447,15 @@
             pltpu.VMEM((64, 16, AHALF), BF16),
             pltpu.VMEM((64, 16, BHALF), BF16),
             pltpu.VMEM((7, 8, 16, AHALF), BF16),
-            pltpu.VMEM((HALVES, 7, NP, 16, BHALF), BF16),
+            pltpu.VMEM((7, NZ, 16, BHALF), BF16),
             pltpu.VMEM((8, 16, AHALF), F32),
-            pltpu.VMEM((HALVES, NP, 16, BHALF), F32),
+            pltpu.VMEM((NZ, 16, BHALF), F32),
             pltpu.VMEM((8, 16, AHALF), BF16),
             pltpu.VMEM((8, 16, BHALF), BF16),
             pltpu.VMEM((7, 16, AHALF), BF16),
             pltpu.VMEM((7, 16, BHALF), BF16),
-            dma((CHUNKS + 2,)), dma((2,)), dma((2,)), dma((3,)), dma((3,)),
-            dma((7,)), dma((7,)), dma((14,)), dma((14,)), dma((7,)), dma((7,)), dma((7,)), dma((7,)),
+            dma((CHUNKS + 2,)), dma((2,)), dma((2,)), dma((len(GROUPS) + 1,)), dma((len(GROUPS) + 1,)),
+            dma((7,)), dma((7,)), dma((len(GROUPS) * 7,)), dma((len(GROUPS) * 7,)), dma((7,)), dma((7,)), dma((7,)), dma((7,)),
         ],
         compiler_params=pltpu.CompilerParams(
             collective_id=0, has_side_effects=True, vmem_limit_bytes=56 * 1024 * 1024

time: 33.6 us -> 33.3 us (level)
  no operation moved by 1% of the time
where the time goes in v7:
time: 33.3 us; the launch traced here: 33.2 us
  Pallas kernels  32.6 us (98%)
  between operations  0.64 us (2%)
    pallas_call x1, Pallas kernels, shards(): pl.pallas_call(kernel, out_shape=pltpu.VMEM((8, WIDTH), F32), in_specs=[p...  31.8 us
    pallas_call x1, Pallas kernels, shards(): pl.pallas_call(outputs, out_shape=(jax.ShapeDtypeStruct((8, WIDTH), F32),...  0.72 us

profile of v7, /device:TPU:1, one launch (start us, length us, event | category | flops | bytes accessed | tf_op | source)
XLA Modules:
  0.0 33.2 jit_solution(17489620181636302197)
XLA Ops:
  0.6 31.8 %shard_map.50.rows_ref = f32[8,1024]{1,0:T(8,128)S(1)} custom-call(bf16[2048,1024]{1,0:T(8,128)(2,1)} %jac.1, bf16[16,128]{1,0:T(8,128)(2,1)} %bitcast.3, f32[1,64]{1,0:T(1,128)} %bitcast.4), custom_call_target="tpu_custom_call" | custom-call | tf_op jit(solution)/shard_map/pallas_call | solution.py:427
  32.5 0.7 %shard_map.51 = (f32[8,1024]{1,0:T(8,128)}, f32[1,8]{1,0:T(1,128)}) custom-call(f32[8,1024]{1,0:T(8,128)S(1)} %shard_map.50.rows_ref), custom_call_target="tpu_custom_call" | custom-call | tf_op jit(solution)/shard_map/pallas_call | solution.py:464

commit v8 on v7

--- a/solution.py
+++ b/solution.py
@@ -26,7 +26,7 @@
 Z_STEPS = [4, 3, 5, 2, 6, 1, 7]
 GROUPS = [(0, 4), (4, 8)]
 PLAN = [("gram", "a"), ("send", 0), ("send", "a"), ("gram", 1), ("send", 1)]
-PASSES = [0, "a", 1]
+PASSES = ["a", 0, 1]
 
 
 def position(x, z, y, c):

time: 33.3 us -> 33.3 us (level)
  no operation moved by 1% of the time
where the time goes in v8:
time: 33.3 us; the launch traced here: 33.2 us
  Pallas kernels  32.6 us (98%)
  between operations  0.64 us (2%)
    pallas_call x1, Pallas kernels, shards(): pl.pallas_call(kernel, out_shape=pltpu.VMEM((8, WIDTH), F32), in_specs=[p...  31.8 us
    pallas_call x1, Pallas kernels, shards(): pl.pallas_call(outputs, out_shape=(jax.ShapeDtypeStruct((8, WIDTH), F32),...  0.72 us

profile of v8, /device:TPU:1, one launch (start us, length us, event | category | flops | bytes accessed | tf_op | source)
XLA Modules:
  0.0 33.2 jit_solution(13961526166552448886)
XLA Ops:
  0.6 31.8 %shard_map.50.rows_ref = f32[8,1024]{1,0:T(8,128)S(1)} custom-call(bf16[2048,1024]{1,0:T(8,128)(2,1)} %jac.1, bf16[16,128]{1,0:T(8,128)(2,1)} %bitcast.3, f32[1,64]{1,0:T(1,128)} %bitcast.4), custom_call_target="tpu_custom_call" | custom-call | tf_op jit(solution)/shard_map/pallas_call | solution.py:427
  32.5 0.7 %shard_map.51 = (f32[8,1024]{1,0:T(8,128)}, f32[1,8]{1,0:T(1,128)}) custom-call(f32[8,1024]{1,0:T(8,128)S(1)} %shard_map.50.rows_ref), custom_call_target="tpu_custom_call" | custom-call | tf_op jit(solution)/shard_map/pallas_call | solution.py:464
